TPU v7x, 32 devices: a whole 2x2x4 slice. The times are simulated.
32 devices in a mesh: dp: 8 (over z, x), img: 4 (over y, core).
Axes of the slice: x: 2, y: 2, z: 4, core: 2. Of those that a mesh axis runs over, the one named last changes fastest.
Arguments:
- image: bfloat16 [8, 16, 64, 512], P('dp', 'img'), may hold values from -6 to 6
- cond: bfloat16 [8, 2048], P('dp'), may hold values from -6 to 6
- context: bfloat16 [8, 81, 2048], P('dp'), may hold values from -6 to 6
- w_conv1: bfloat16 [4608, 512], P(('dp', 'img')), may hold values from -0.09375 to 0.09375
- w_conv2: bfloat16 [4608, 512], P(('dp', 'img')), may hold values from -0.09375 to 0.09375
- w_embed: bfloat16 [2048, 1024], P(('dp', 'img')), may hold values from -0.125 to 0.125
- w_qkv: bfloat16 [512, 1536], P(('dp', 'img')), may hold values from -0.25 to 0.25
- w_context: bfloat16 [2048, 1024], P(('dp', 'img')), may hold values from -0.125 to 0.125
- w_out: bfloat16 [512, 512], P(('dp', 'img')), may hold values from -6 to 6
- vectors: bfloat16 [16, 512], P(None, ('dp', 'img')), may hold values from -1.5 to 1.75, as said below
- cotangent: bfloat16 [8, 16, 64, 512], P('dp', 'img'), may hold values from -6 to 6
Outputs:
- output: bfloat16 [8, 16, 64, 512], P('dp', 'img')
- in_grad: bfloat16 [8, 16, 64, 512], P('dp', 'img')
- g_conv1: float32 [4608, 512], P(('dp', 'img'))
- g_conv2: float32 [4608, 512], P(('dp', 'img'))
- g_embed: float32 [2048, 1024], P(('dp', 'img'))
- g_qkv: float32 [512, 1536], P(('dp', 'img'))
- g_context: float32 [2048, 1024], P(('dp', 'img'))
- g_out: float32 [512, 512], P(('dp', 'img'))
- g_vectors: float32 [16, 512], P(None, ('dp', 'img'))
Inputs may be any that keep to these rules, and one draw needn't show every extreme that they name: `vectors`: rows 0, 3 and 6 lie between 0.25 and 1.75, the others between -1.5 and 1.5.
All inputs are finite; a program needn't handle non-finite values.
Results may differ from a plain program's by a relative error of at most 0.014.
Values may be sent and summed in bfloat16 or wider, within the bound.
A program may use at most 192 MiB of HBM per device.

v0:
```python
import jax
import jax.numpy as jnp
from jax import lax
from jax.sharding import PartitionSpec as P

HEADS = 8
HEAD = 64
GROUPS = 32


highest = lax.Precision.HIGHEST


def with_halo(block, sides, width):
    for axis, dim in sides:
        count = lax.axis_size(axis)
        forward = [(i, i + 1) for i in range(count - 1)]
        backward = [(target, source) for source, target in forward]
        low = lax.ppermute(
            lax.slice_in_dim(block, block.shape[dim] - width, None, axis=dim), axis, forward
        )
        high = lax.ppermute(lax.slice_in_dim(block, 0, width, axis=dim), axis, backward)
        block = jnp.concatenate([low, block, high], axis=dim)
    return block


def silu_slope(value):
    sigma = jax.nn.sigmoid(value)
    return sigma * (1.0 + value * (1.0 - sigma))


def group_moments(flat):
    pixels, chans = flat.shape
    part = flat.reshape(pixels, GROUPS, chans // GROUPS)
    sums, squares = lax.psum((jnp.sum(part, axis=(0, 2)), jnp.sum(part * part, axis=(0, 2))), "img")
    count = pixels * (chans // GROUPS) * lax.axis_size("img")
    mean = sums / count
    inverse = lax.rsqrt(squares / count - mean * mean + 1e-05)
    normed = (part - mean[None, :, None]) * inverse[None, :, None]
    return (normed.reshape(pixels, chans), inverse)


def group_back(grad_hat, normed, inverse):
    pixels, chans = grad_hat.shape
    upper = grad_hat.reshape(pixels, GROUPS, chans // GROUPS)
    lower = normed.reshape(pixels, GROUPS, chans // GROUPS)
    first, second = lax.psum(
        (jnp.sum(upper, axis=(0, 2)), jnp.sum(upper * lower, axis=(0, 2))), "img"
    )
    count = pixels * (chans // GROUPS) * lax.axis_size("img")
    result = (
        upper - first[None, :, None] / count - lower * (second[None, :, None] / count)
    ) * inverse[None, :, None]
    return result.reshape(pixels, chans)


def patches(padded, rows, cols, flipped):
    pieces = []
    for row_tap in range(3):
        for col_tap in range(3):
            top = 2 - row_tap if flipped else row_tap
            left = 2 - col_tap if flipped else col_tap
            pieces.append(padded[top : top + rows, left : left + cols])
    stacked = jnp.stack(pieces, axis=2)
    return stacked.reshape(rows * cols, 9, padded.shape[-1])


def conv_forward(field, kernel):
    rows, cols, chans = field.shape
    rimmed = with_halo(field, (("img", 0),), 1)
    padded = jnp.pad(rimmed, ((0, 0), (1, 1), (0, 0)))
    taps = patches(padded, rows, cols, False)
    result = jnp.dot(
        taps.reshape(rows * cols, 9 * chans), kernel, preferred_element_type=jnp.float32
    )
    return (result, taps)


def conv_backward(grad, kernel, taps):
    rows, cols, chans = grad.shape
    rimmed = with_halo(grad, (("img", 0),), 1)
    padded = jnp.pad(rimmed, ((0, 0), (1, 1), (0, 0)))
    back_taps = patches(padded, rows, cols, True)
    kernel3 = kernel.reshape(9, kernel.shape[0] // 9, kernel.shape[1])
    grad_in = jnp.einsum("ptc,tdc->pd", back_taps, kernel3, preferred_element_type=jnp.float32)
    flat_grad = grad.reshape(rows * cols, chans)
    grad_kernel = jnp.einsum(
        "pk,pc->kc",
        taps.reshape(rows * cols, 9 * chans),
        flat_grad,
        preferred_element_type=jnp.float32,
    )
    return (grad_in, grad_kernel)


def head_forward(inputs):
    query, keys, values = inputs
    factor = query.shape[-1] ** (-0.5)
    scores = jnp.einsum("pd,kd->pk", query, keys, preferred_element_type=jnp.float32) * factor
    top = jnp.max(scores, axis=1, keepdims=True)
    weights = jnp.exp(scores - top)
    total = jnp.sum(weights, axis=1, keepdims=True)
    probs = (weights / total).astype(jnp.bfloat16)
    mixed = jnp.dot(probs, values, preferred_element_type=jnp.float32)
    return (mixed, top[:, 0] + jnp.log(total[:, 0]))


def head_backward(inputs):
    query, keys, values, grad_out, logsum = inputs
    factor = query.shape[-1] ** (-0.5)
    scores = jnp.einsum("pd,kd->pk", query, keys, preferred_element_type=jnp.float32) * factor
    probs = jnp.exp(scores - logsum[:, None])
    probs_low = probs.astype(jnp.bfloat16)
    grad_values = jnp.einsum("pk,pd->kd", probs_low, grad_out, preferred_element_type=jnp.float32)
    grad_probs = jnp.einsum("pd,kd->pk", grad_out, values, preferred_element_type=jnp.float32)
    inner = jnp.sum(grad_probs * probs, axis=1, keepdims=True)
    grad_scores = (probs * (grad_probs - inner)).astype(jnp.bfloat16)
    grad_query = jnp.dot(grad_scores, keys, preferred_element_type=jnp.float32) * factor
    grad_keys = (
        jnp.einsum("pk,pd->kd", grad_scores, query, preferred_element_type=jnp.float32) * factor
    )
    return (grad_query, grad_keys, grad_values)


def split_heads(matrix):
    return matrix.reshape(matrix.shape[0], HEADS, HEAD).transpose(1, 0, 2)


def merge_heads(stacked):
    return stacked.transpose(1, 0, 2).reshape(stacked.shape[1], HEADS * HEAD)


def on_device(
    image, cond, context, w_conv1, w_conv2, w_embed, w_qkv, w_context, w_out, vectors, cotangent
):
    conv1_full, conv2_full, embed_full, vec_low, qkv_full, context_full, out_full = (
        lax.all_gather(w_conv1, ("dp", "img"), axis=0, tiled=True),
        lax.all_gather(w_conv2, ("dp", "img"), axis=0, tiled=True),
        lax.all_gather(w_embed, ("dp", "img"), axis=0, tiled=True),
        lax.all_gather(vectors, ("dp", "img"), axis=1, tiled=True),
        lax.all_gather(w_qkv, ("dp", "img"), axis=0, tiled=True),
        lax.all_gather(w_context, ("dp", "img"), axis=0, tiled=True),
        lax.all_gather(w_out, ("dp", "img"), axis=0, tiled=True),
    )
    vec = vec_low.astype(jnp.float32)
    rows, cols, chans = (image.shape[1], image.shape[2], image.shape[3])
    pixels = rows * cols
    flat = image[0].reshape(pixels, chans).astype(jnp.float32)
    normed1, inverse1 = group_moments(flat)
    pre1 = normed1 * vec[0] + vec[1]
    act1 = jax.nn.silu(pre1).astype(jnp.bfloat16)
    conv1, taps1 = conv_forward(act1.reshape(rows, cols, chans), conv1_full)
    hidden1 = conv1 + vec[2]
    cond_act = jax.nn.silu(cond.astype(jnp.float32)).astype(jnp.bfloat16)
    embed = jnp.dot(cond_act, embed_full, preferred_element_type=jnp.float32)[0]
    scale = embed[:chans] + vec[14]
    shift = embed[chans:] + vec[15]
    normed2, inverse2 = group_moments(hidden1)
    affine2 = normed2 * vec[3] + vec[4]
    pre2 = affine2 * (1.0 + scale) + shift
    act2 = jax.nn.silu(pre2).astype(jnp.bfloat16)
    conv2, taps2 = conv_forward(act2.reshape(rows, cols, chans), conv2_full)
    resid = flat + conv2 + vec[5]
    normed3, inverse3 = group_moments(resid)
    affine3 = (normed3 * vec[6] + vec[7]).astype(jnp.bfloat16)
    proj_bias = jnp.concatenate([vec[9], vec[10], vec[11]])
    proj = (jnp.dot(affine3, qkv_full, preferred_element_type=jnp.float32) + proj_bias).astype(
        jnp.bfloat16
    )
    image_kv = lax.all_gather(proj[:, chans:], "img", axis=0, tiled=True)
    ctx_bias = jnp.concatenate([vec[12], vec[13]])
    ctx_kv = (
        jnp.dot(context[0], context_full, preferred_element_type=jnp.float32) + ctx_bias
    ).astype(jnp.bfloat16)
    keys = jnp.concatenate([ctx_kv[:, :chans], image_kv[:, :chans]], 0)
    values = jnp.concatenate([ctx_kv[:, chans:], image_kv[:, chans:]], 0)
    query_heads = split_heads(proj[:, :chans])
    key_heads = split_heads(keys)
    value_heads = split_heads(values)
    mixed, logsum = lax.map(head_forward, (query_heads, key_heads, value_heads))
    mixed_low = merge_heads(mixed).astype(jnp.bfloat16)
    attended = jnp.dot(mixed_low, out_full, preferred_element_type=jnp.float32) + vec[8]
    output = (resid + attended).astype(jnp.bfloat16).reshape(image.shape)
    conv1_full, conv2_full, embed_full, vec_low, qkv_full, context_full, out_full = (
        lax.all_gather(w_conv1, ("dp", "img"), axis=0, tiled=True),
        lax.all_gather(w_conv2, ("dp", "img"), axis=0, tiled=True),
        lax.all_gather(w_embed, ("dp", "img"), axis=0, tiled=True),
        lax.all_gather(vectors, ("dp", "img"), axis=1, tiled=True),
        lax.all_gather(w_qkv, ("dp", "img"), axis=0, tiled=True),
        lax.all_gather(w_context, ("dp", "img"), axis=0, tiled=True),
        lax.all_gather(w_out, ("dp", "img"), axis=0, tiled=True),
    )
    vec = vec_low.astype(jnp.float32)
    grad_top = cotangent[0].reshape(pixels, chans)
    grad_top_wide = grad_top.astype(jnp.float32)
    grad_mixed = jnp.einsum(
        "pc,dc->pd", grad_top, out_full, preferred_element_type=jnp.float32
    ).astype(jnp.bfloat16)
    grad_out_w = jnp.einsum("pd,pc->dc", mixed_low, grad_top, preferred_element_type=jnp.float32)
    grad_heads = split_heads(grad_mixed)
    ctx_count = ctx_kv.shape[0]
    grad_query, grad_keys, grad_values = lax.map(
        head_backward, (query_heads, key_heads, value_heads, grad_heads, logsum)
    )
    grad_query = merge_heads(grad_query)
    grad_keys = merge_heads(grad_keys)
    grad_values = merge_heads(grad_values)
    grad_ctx = jnp.concatenate([grad_keys[:ctx_count], grad_values[:ctx_count]], 1)
    image_terms = jnp.concatenate([grad_keys[ctx_count:], grad_values[ctx_count:]], 1)
    own_kv = lax.psum_scatter(
        image_terms.astype(jnp.bfloat16), "img", scatter_dimension=0, tiled=True
    ).astype(jnp.float32)
    grad_proj = jnp.concatenate([grad_query, own_kv], 1).astype(jnp.bfloat16)
    grad_proj_wide = grad_proj.astype(jnp.float32)
    grad_qkv_w = jnp.einsum("pc,pk->ck", affine3, grad_proj, preferred_element_type=jnp.float32)
    grad_context_w = jnp.einsum(
        "kx,kc->xc",
        context[0].astype(jnp.float32),
        grad_ctx,
        precision=highest,
        preferred_element_type=jnp.float32,
    )
    grad_affine3 = jnp.einsum("pk,ck->pc", grad_proj, qkv_full, preferred_element_type=jnp.float32)
    grad_resid = grad_top_wide + group_back(grad_affine3 * vec[6], normed3, inverse3)
    grad_hidden2 = grad_resid.astype(jnp.bfloat16)
    grad_act2, grad_conv2 = conv_backward(
        grad_hidden2.reshape(rows, cols, chans), conv2_full, taps2
    )
    grad_pre2 = grad_act2 * silu_slope(pre2)
    grad_scale = jnp.sum(grad_pre2 * affine2, axis=0)
    grad_shift = jnp.sum(grad_pre2, axis=0)
    grad_affine2 = grad_pre2 * (1.0 + scale)
    grad_hidden1 = group_back(grad_affine2 * vec[3], normed2, inverse2).astype(jnp.bfloat16)
    grad_act1, grad_conv1 = conv_backward(
        grad_hidden1.reshape(rows, cols, chans), conv1_full, taps1
    )
    grad_pre1 = grad_act1 * silu_slope(pre1)
    in_grad = (
        (grad_resid + group_back(grad_pre1 * vec[0], normed1, inverse1))
        .astype(jnp.bfloat16)
        .reshape(image.shape)
    )
    grad_embed = jnp.concatenate([grad_scale, grad_shift])
    proj_sums = jnp.sum(grad_proj_wide, axis=0)
    ctx_sums = jnp.sum(grad_ctx, axis=0)
    grad_vec = jnp.stack(
        [
            jnp.sum(grad_pre1 * normed1, axis=0),
            jnp.sum(grad_pre1, axis=0),
            jnp.sum(grad_hidden1.astype(jnp.float32), axis=0),
            jnp.sum(grad_affine2 * normed2, axis=0),
            jnp.sum(grad_affine2, axis=0),
            jnp.sum(grad_hidden2.astype(jnp.float32), axis=0),
            jnp.sum(grad_affine3 * normed3, axis=0),
            jnp.sum(grad_affine3, axis=0),
            jnp.sum(grad_top_wide, axis=0),
            proj_sums[:chans],
            proj_sums[chans : 2 * chans],
            proj_sums[2 * chans :],
            ctx_sums[:chans],
            ctx_sums[chans:],
            grad_scale,
            grad_shift,
        ],
        0,
    )
    grad_embed_w = cond_act[0].astype(jnp.float32)[:, None] * grad_embed[None, :]
    g_conv1, g_conv2, g_embed, g_vectors = (
        lax.psum_scatter(grad_conv1, ("dp", "img"), scatter_dimension=0, tiled=True),
        lax.psum_scatter(grad_conv2, ("dp", "img"), scatter_dimension=0, tiled=True),
        lax.psum_scatter(grad_embed_w, ("dp", "img"), scatter_dimension=0, tiled=True),
        lax.psum_scatter(grad_vec, ("dp", "img"), scatter_dimension=1, tiled=True),
    )
    g_qkv, g_context, g_out = (
        lax.psum_scatter(grad_qkv_w, ("dp", "img"), scatter_dimension=0, tiled=True),
        lax.psum_scatter(grad_context_w, ("dp", "img"), scatter_dimension=0, tiled=True),
        lax.psum_scatter(grad_out_w, ("dp", "img"), scatter_dimension=0, tiled=True),
    )
    return (output, in_grad, g_conv1, g_conv2, g_embed, g_qkv, g_context, g_out, g_vectors)


def solution(mesh):
    in_specs = (
        P("dp", "img", None, None),
        P("dp", None),
        P("dp", None, None),
        P(("dp", "img"), None),
        P(("dp", "img"), None),
        P(("dp", "img"), None),
        P(("dp", "img"), None),
        P(("dp", "img"), None),
        P(("dp", "img"), None),
        P(None, ("dp", "img")),
        P("dp", "img", None, None),
    )
    out_specs = (
        P("dp", "img", None, None),
        P("dp", "img", None, None),
        P(("dp", "img"), None),
        P(("dp", "img"), None),
        P(("dp", "img"), None),
        P(("dp", "img"), None),
        P(("dp", "img"), None),
        P(("dp", "img"), None),
        P(None, ("dp", "img")),
    )
    return jax.shard_map(
        on_device, mesh=mesh, in_specs=in_specs, out_specs=out_specs, check_vma=False
    )
```

profile of v0, /device:TPU:0, one launch (start us, length us, event | category | flops | bytes accessed | tf_op | source)
XLA Modules:
  0.0 1496.4 jit_solution(3816116527417239734)
XLA Ops:
  12.1 8.4 all-reduce.9
  21.5 41.6 %all_gather.29 = bf16[16,512]{0,1:T(8,128)(2,1)S(1)} all-gather(bf16[16,16]{0,1:T(8,128)(2,1)S(1)} %copy.75), channel_id=1, replica_groups=mesh['dp'=8,'img'=4] {'dp','img'}, dimensions={1}, use_global_device_ids=true | all-gather | bytes 16896 | tf_op jit(solution)/shard_map/all_gather | solution.py:140
  79.8 61.5 %all-gather.7.cloned.1.call-done = bf16[4608,512]{1,0:T(8,128)(2,1)} async-done(((bf16[144,512]{1,0:T(8,128)(2,1)}), bf16[4608,512]{1,0:T(8,128)(2,1)}) %all-gather.7.cloned.1.call-update) | async-done | bytes 4718608 | tf_op jit(solution)/shard_map/all_gather | solution.py:137
  147.3 7.0 all-reduce.8
  164.8 41.7 %all-gather.11.cloned.1.call-done = bf16[4608,512]{1,0:T(8,128)(2,1)} async-done(((bf16[144,512]{1,0:T(8,128)(2,1)}), bf16[4608,512]{1,0:T(8,128)(2,1)}) %all-gather.11.cloned.1.call-update) | async-done | bytes 4718608 | tf_op jit(solution)/shard_map/all_gather | solution.py:138
  210.8 7.0 all-reduce.7
  218.1 45.1 %all-gather.13.cloned.1.call-done = bf16[512,1536]{1,0:T(8,128)(2,1)} async-done(((bf16[16,1536]{1,0:T(8,128)(2,1)}), bf16[512,1536]{1,0:T(8,128)(2,1)}) %all-gather.13.cloned.1.call-update) | async-done | bytes 1572880 | tf_op jit(solution)/shard_map/all_gather | solution.py:141
  266.3 41.3 %all_gather.36 = bf16[512,512]{1,0:T(8,128)(2,1)S(1)} all-gather(bf16[16,512]{1,0:T(8,128)(2,1)S(1)} %copy-done.42), channel_id=1, replica_groups=mesh['dp'=8,'img'=4] {'dp','img'}, dimensions={0}, use_global_device_ids=true | all-gather | bytes 540672 | tf_op jit(solution)/shard_map/all_gather | solution.py:143
  309.6 17.6 %all-gather.15.cloned.1.call-done = bf16[2048,1024]{1,0:T(8,128)(2,1)} async-done(((bf16[64,1024]{1,0:T(8,128)(2,1)}), bf16[2048,1024]{1,0:T(8,128)(2,1)}) %all-gather.15.cloned.1.call-update) | async-done | bytes 4194320 | tf_op jit(solution)/shard_map/all_gather | solution.py:142
  331.4 18.4 %all-gather.17.cloned.1.call-done = bf16[1024,1024]{1,0:T(8,128)(2,1)} async-done(((bf16[256,1024]{1,0:T(8,128)(2,1)}), bf16[1024,1024]{1,0:T(8,128)(2,1)}) %all-gather.17.cloned.1.call-update) | async-done | bytes 2097168 | tf_op jit(solution)/shard_map/all_gather | solution.py:170
  364.1 27.5 %while.26 = (s32[]{:T(128)}, bf16[8,256,64]{1,2,0:T(8,128)(2,1)}, f32[8,256]{1,0:T(8,128)S(1)}, bf16[8,256,64]{2,1,0:T(8,128)(2,1)}, bf16[8,1105,64]{2,1,0:T(8,1...) while((s32[]{:T(128)}, bf16[8,256,64]{1,2,0:T(8,128)(2,1)}, ...), condition=%wide.region_21.22_spmd, body=%wide.region_18.21_spmd.sunk | while | flops 74397184 | bytes 4107361 | solution.py:180
  392.3 59.4 %while.27 = (s32[]{:T(128)}, bf16[8,256,64]{1,2,0:T(8,128)(2,1)}, f32[8,1105,64]{1,2,0:T(8,128)}, f32[8,1105,64]{1,2,0:T(8,128)}, bf16[8,256,64]{2,1,0:T(8,128)(...) while((s32[]{:T(128)}, bf16[8,256,64]{1,2,0:T(8,128)(2,1)}, ...), condition=%wide.region_24.25_spmd, body=%wide.region_22.24_spmd.sunk | while | flops 183393088 | bytes 10206321 | solution.py:202
  461.3 27.9 %reduce-scatter.13.cloned.1.call-done = bf16[256,1024]{0,1:T(8,128)(2,1)} async-done(((bf16[1024,1024]{0,1:T(8,128)(2,1)}), bf16[256,1024]{0,1:T(8,128)(2,1)}) %reduce-scatter.13.cloned.1.call-update) | async-done | bytes 524304 | tf_op jit(solution)/shard_map/reduce_scatter | solution.py:210
  492.5 5.8 all-reduce.6
  510.1 8.6 all-reduce.5
  551.1 9.3 copy.91
  574.2 8.6 all-reduce.4
  584.2 86.0 %reduce-scatter.27.cloned.1.call-done = f32[16,16]{1,0:T(8,128)} async-done(((f32[512,16]{1,0:T(8,128)}), f32[16,16]{1,0:T(8,128)}) %reduce-scatter.27.cloned.1.call-update) | async-done | bytes 1040
  671.6 132.1 %reduce-scatter.23.cloned.1.call-done = f32[16,512]{1,0:T(8,128)} async-done(((f32[512,512]{1,0:T(8,128)}), f32[16,512]{1,0:T(8,128)}) %reduce-scatter.23.cloned.1.call-update) | async-done | bytes 32784 | tf_op jit(solution)/shard_map/reduce_scatter | solution.py:277
  803.8 104.2 %reduce-scatter.21.cloned.1.call-done = f32[16,1536]{1,0:T(8,128)} async-done(((f32[512,1536]{1,0:T(8,128)}), f32[16,1536]{1,0:T(8,128)}) %reduce-scatter.21.cloned.1.call-update) | async-done | bytes 98320 | tf_op jit(solution)/shard_map/reduce_scatter | solution.py:275
  907.9 142.1 %reduce-scatter.17.cloned.1.call-done = f32[144,512]{1,0:T(8,128)} async-done(((f32[4608,512]{1,0:T(8,128)}), f32[144,512]{1,0:T(8,128)}) %reduce-scatter.17.cloned.1.call-update) | async-done | bytes 294928 | tf_op jit(solution)/shard_map/reduce_scatter | solution.py:270
  1050.1 150.8 %reduce-scatter.25.cloned.1.call-done = f32[64,1024]{1,0:T(8,128)} async-done(((f32[2048,1024]{1,0:T(8,128)}), f32[64,1024]{1,0:T(8,128)}) %reduce-scatter.25.cloned.1.call-update) | async-done | bytes 262160
  1200.9 137.9 %reduce-scatter.15.cloned.1.call-done = f32[144,512]{1,0:T(8,128)} async-done(((f32[4608,512]{1,0:T(8,128)}), f32[144,512]{1,0:T(8,128)}) %reduce-scatter.15.cloned.1.call-update) | async-done | bytes 294928 | tf_op jit(solution)/shard_map/reduce_scatter | solution.py:269
  1338.8 150.9 %reduce-scatter.19.cloned.1.call-done = f32[64,1024]{1,0:T(8,128)} async-done(((f32[2048,1024]{1,0:T(8,128)}), f32[64,1024]{1,0:T(8,128)}) %reduce-scatter.19.cloned.1.call-update) | async-done | bytes 262160 | tf_op jit(solution)/shard_map/reduce_scatter | solution.py:271
  (455 shorter events, 226.8 us)
Async XLA Ops:
  7.2 320.0 %copy-start = (bf16[1,81,2048]{2,1,0:T(8,128)(2,1)S(1)}, bf16[1,81,2048]{2,1,0:T(8,128)(2,1)}, u32[]{:S(2)}) copy-start(bf16[1,81,2048]{2,1,0:T(8,128)(2,1)} %param.17) | copy-start | bytes 995332
  7.2 68.9 %all-gather.9.cloned.1.call-start = ((), (), s32[]{:S(2)}) async-start(), calls=%async_computation.9 | async-start | bytes 4325376 | tf_op jit(solution)/shard_map/all_gather | solution.py:139
  7.9 133.3 %all-gather.7.cloned.1.call-start = ((), (), s32[]{:S(2)}) async-start(), calls=%async_computation.8 | async-start | bytes 4866048 | tf_op jit(solution)/shard_map/all_gather | solution.py:137
  8.7 197.9 %all-gather.11.cloned.1.call-start = ((), (), s32[]{:S(2)}) async-start(), calls=%async_computation.10 | async-start | bytes 4866048 | tf_op jit(solution)/shard_map/all_gather | solution.py:138
  9.4 253.8 %all-gather.13.cloned.1.call-start = ((), (), s32[]{:S(2)}) async-start(), calls=%async_computation.11 | async-start | bytes 1622016 | tf_op jit(solution)/shard_map/all_gather | solution.py:141
  10.0 317.2 %all-gather.15.cloned.1.call-start = ((), (), s32[]{:S(2)}) async-start(), calls=%async_computation.12 | async-start | bytes 4325376 | tf_op jit(solution)/shard_map/all_gather | solution.py:142
  10.6 339.2 %all-gather.17.cloned.1.call-start = ((), (), s32[]{:S(2)}) async-start(), calls=%async_computation.13 | async-start | bytes 2621440 | tf_op jit(solution)/shard_map/all_gather | solution.py:170
  63.8 199.4 %copy-start.44 = (f32[1,512]{1,0:T(1,128)}, f32[1,512]{1,0:T(1,128)S(1)}, u32[]{:S(2)}) copy-start(f32[1,512]{1,0:T(1,128)S(1)} %get-tuple-element.305) | copy-start | bytes 6148
  65.9 3.8 collective-permute-start
  68.1 3.1 collective-permute-start.1
  154.9 3.8 collective-permute-start.2
  156.3 3.9 collective-permute-start.3
  266.2 223.0 %reduce-scatter.13.cloned.1.call-start = ((), (), s32[]{:S(2)}) async-start(), calls=%async_computation.14 | async-start | bytes 2621440 | tf_op jit(solution)/shard_map/reduce_scatter | solution.py:210
  457.6 212.6 %reduce-scatter.27.cloned.1.call-start = ((), (), s32[]{:S(2)}) async-start(), calls=%async_computation.21 | async-start | bytes 270336
  499.4 4.0 collective-permute-start.4
  501.2 4.6 collective-permute-start.5
  519.8 2.9 collective-permute-start.6
  521.2 4.9 collective-permute-start.7
  534.0 269.7 %reduce-scatter.23.cloned.1.call-start = ((), (), s32[]{:S(2)}) async-start(), calls=%async_computation.19 | async-start | bytes 1081344 | tf_op jit(solution)/shard_map/reduce_scatter | solution.py:277
  535.4 372.6 %reduce-scatter.21.cloned.1.call-start = ((), (), s32[]{:S(2)}) async-start(), calls=%async_computation.18 | async-start | bytes 3244032 | tf_op jit(solution)/shard_map/reduce_scatter | solution.py:275
  537.8 512.3 %reduce-scatter.17.cloned.1.call-start = ((), (), s32[]{:S(2)}) async-start(), calls=%async_computation.16 | async-start | bytes 9732096 | tf_op jit(solution)/shard_map/reduce_scatter | solution.py:270
  544.5 656.4 %reduce-scatter.25.cloned.1.call-start = ((), (), s32[]{:S(2)}) async-start(), calls=%async_computation.20 | async-start | bytes 8650752
  560.4 778.4 %reduce-scatter.15.cloned.1.call-start = ((), (), s32[]{:S(2)}) async-start(), calls=%async_computation.15 | async-start | bytes 9732096 | tf_op jit(solution)/shard_map/reduce_scatter | solution.py:269
  567.2 922.5 %reduce-scatter.19.cloned.1.call-start = ((), (), s32[]{:S(2)}) async-start(), calls=%async_computation.17 | async-start | bytes 8650752 | tf_op jit(solution)/shard_map/reduce_scatter | solution.py:271
  (68 other events, 1052.5 us)
Sparse Core Ops, SparseCore 0:
  10.9 65.1 all-gather.8
  79.0 62.1 all-gather.6
  144.2 62.3 all-gather.10
  209.3 53.8 all-gather.12
  265.9 61.2 all-gather.14
  328.6 21.1 all-gather.16
  457.7 31.4 reduce-scatter.12
  534.1 136.0 reduce-scatter.26
  673.1 130.6 reduce-scatter.22
  810.5 97.4 reduce-scatter.20
  915.4 134.5 reduce-scatter.16
  1052.8 148.0 reduce-scatter.24
  1207.4 131.3 reduce-scatter.14
  1341.6 147.9 reduce-scatter.18
where the time goes:
time: 1510 us; the launch traced here: 1500 us
  waiting for transfers between devices  1130 us (75%)
  matrix products  130 us (9%)
  blocking collectives  128 us (8%)
  local copies, waits for them, and re-layouts  59.4 us (4%)
  other arithmetic  21.3 us (1%)
  between operations  15.5 us (1%)
    unnamed x16, waiting for transfers between devices  240 us
    reduce_scatter x1, waiting for transfers between devices, on_device(): lax.psum_scatter(grad_embed_w, ('dp', 'img'), scatter_dimension=0, tiled=...  151 us
    reduce_scatter x1, waiting for transfers between devices, on_device(): lax.psum_scatter(grad_conv2, ('dp', 'img'), scatter_dimension=0, tiled=True)  142 us
    reduce_scatter x1, waiting for transfers between devices, on_device(): lax.psum_scatter(grad_conv1, ('dp', 'img'), scatter_dimension=0, tiled=True)  138 us
    reduce_scatter x1, waiting for transfers between devices, on_device(): lax.psum_scatter(grad_out_w, ('dp', 'img'), scatter_dimension=0, tiled=True)  132 us
    reduce_scatter x1, waiting for transfers between devices, on_device(): lax.psum_scatter(grad_qkv_w, ('dp', 'img'), scatter_dimension=0, tiled=True)  104 us
    all_gather x1, waiting for transfers between devices, on_device(): lax.all_gather(w_conv1, ('dp', 'img'), axis=0, tiled=True)  61.5 us
    all_gather x1, waiting for transfers between devices, on_device(): lax.all_gather(w_qkv, ('dp', 'img'), axis=0, tiled=True)  45.1 us
  transfers between devices with their start and end apart: 22, of which 18 were waited for; matrix products, arithmetic and copies ran while one was open for 5% of the time, Pallas kernels for 0%

commit v1 on v0

v1 whole, which is shorter than its diff:
```python
import jax
import jax.numpy as jnp
from jax import lax
from jax.sharding import PartitionSpec as P

HEADS = 8
HEAD = 64
GROUPS = 32

f32 = jnp.float32
bf16 = jnp.bfloat16
highest = lax.Precision.HIGHEST


def dot(a, b):
    return jnp.dot(a, b, preferred_element_type=f32)


def silu_slope(value):
    sigma = jax.nn.sigmoid(value)
    return sigma * (1.0 + value * (1.0 - sigma))


def group_norm(flat, size):
    pixels, chans = flat.shape
    part = flat.reshape(pixels, chans // size, size)
    mean = jnp.mean(part, axis=(0, 2), keepdims=True)
    spread = jnp.mean(jnp.square(part - mean), axis=(0, 2), keepdims=True)
    inverse = lax.rsqrt(spread + 1e-05)
    return ((part - mean) * inverse).reshape(pixels, chans), inverse


def group_back(grad, normed, inverse, size):
    pixels, chans = grad.shape
    upper = grad.reshape(pixels, chans // size, size)
    lower = normed.reshape(pixels, chans // size, size)
    first = jnp.mean(upper, axis=(0, 2), keepdims=True)
    second = jnp.mean(upper * lower, axis=(0, 2), keepdims=True)
    return ((upper - first - lower * second) * inverse).reshape(pixels, chans)


def taps_of(flat, rows, cols, flipped):
    chans = flat.shape[-1]
    padded = jnp.pad(flat.reshape(rows, cols, chans), ((1, 1), (1, 1), (0, 0)))
    pieces = []
    for r in range(3):
        for c in range(3):
            top, left = (2 - r, 2 - c) if flipped else (r, c)
            pieces.append(padded[top : top + rows, left : left + cols].reshape(rows * cols, chans))
    return jnp.concatenate(pieces, 1)


def columns(weight, parts):
    rows, chans = weight.shape
    return weight.reshape(rows, chans // (parts * 128), parts, 128).transpose(2, 1, 0, 3).reshape(parts, -1, 128)


def on_device(
    image, cond, context, w_conv1, w_conv2, w_embed, w_qkv, w_context, w_out, vectors, cotangent
):
    parts = lax.axis_size("img")
    place = lax.axis_index("img")
    images = lax.axis_size("dp")
    rows, cols, chans = image.shape[1] * parts, image.shape[2], image.shape[3]
    pixels = rows * cols
    width = chans // parts
    size = chans // GROUPS
    count = images * parts

    def own(full):
        return lax.dynamic_slice_in_dim(full, place * width, width, full.ndim - 1)

    shards = (w_conv1, w_conv2, w_qkv, w_context, w_embed, w_out)
    lengths = [w.shape[0] * (w.shape[1] // chans) for w in shards]
    packed = jnp.concatenate([columns(w, parts) for w in shards], 1)
    packed = lax.all_to_all(packed, "img", 0, 0, tiled=True)
    packed = lax.all_gather(packed, "dp", axis=0, tiled=True)
    full = []
    start = 0
    for w, length in zip(shards, lengths):
        wide = w.shape[1] // chans
        piece = packed[:, start : start + length].reshape(count, wide, w.shape[0], width)
        full.append(piece.transpose(0, 2, 1, 3).reshape(count * w.shape[0], wide * width))
        start += length
    k1, k2, kq, kc, ke, ko = full
    vec_all = lax.all_gather(vectors, ("dp", "img"), axis=1, tiled=True).astype(f32)
    vec = own(vec_all)

    x_low = lax.all_gather(image[0].reshape(-1, chans), "img", axis=0, tiled=True)
    x_all = x_low.astype(f32)
    normed1_all, inverse1_all = group_norm(x_all, size)
    act1 = jax.nn.silu(normed1_all * vec_all[0] + vec_all[1]).astype(bf16)
    normed1 = own(normed1_all)
    inverse1 = lax.dynamic_slice_in_dim(inverse1_all, place * (GROUPS // parts), GROUPS // parts, 1)
    pre1 = normed1 * vec[0] + vec[1]
    hidden1 = dot(taps_of(act1, rows, cols, False), k1) + vec[2]
    cond_act = jax.nn.silu(cond.astype(f32)).astype(bf16)
    embed = dot(cond_act, ke)[0]
    scale = embed[:width] + vec[14]
    shift = embed[width:] + vec[15]
    normed2, inverse2 = group_norm(hidden1, size)
    affine2 = normed2 * vec[3] + vec[4]
    pre2 = affine2 * (1.0 + scale) + shift
    act2_own = jax.nn.silu(pre2).astype(bf16)
    act2 = lax.all_gather(act2_own, "img", axis=1, tiled=True)
    resid = own(x_all) + dot(taps_of(act2, rows, cols, False), k2) + vec[5]
    normed3, inverse3 = group_norm(resid, size)
    affine3_own = (normed3 * vec[6] + vec[7]).astype(bf16)
    affine3 = lax.all_gather(affine3_own, "img", axis=1, tiled=True)
    qkv = (dot(affine3, kq) + jnp.concatenate([vec[9], vec[10], vec[11]])).astype(bf16)
    ctx = (dot(context[0], kc) + jnp.concatenate([vec[12], vec[13]])).astype(bf16)
    tokens = ctx.shape[0]

    out_full = lax.all_gather(ko, "img", axis=1, tiled=True)
    dy_px = cotangent[0].reshape(-1, chans)
    do_px = lax.dot_general(dy_px, out_full, (((1,), (1,)), ((), ())), preferred_element_type=f32).astype(bf16)
    both = jnp.stack([do_px, dy_px])
    both = lax.all_to_all(both, "img", 2, 1, tiled=True)
    do, dy = both[0], both[1]
    dy_wide = dy.astype(f32)

    keys = jnp.concatenate([ctx[:, :width], qkv[:, width : 2 * width]], 0)
    values = jnp.concatenate([ctx[:, width:], qkv[:, 2 * width :]], 0)
    factor = HEAD ** (-0.5)
    mixed, dq, dk, dv = [], [], [], []
    for h in range(width // HEAD):
        at = slice(h * HEAD, (h + 1) * HEAD)
        q_h, k_h, v_h, do_h = qkv[:, at], keys[:, at], values[:, at], do[:, at]
        scores = dot(k_h, q_h.T) * factor
        top = jnp.max(scores, 0, keepdims=True)
        weights = jnp.exp(scores - top)
        probs = weights / jnp.sum(weights, 0, keepdims=True)
        low = probs.astype(bf16)
        mixed.append(dot(v_h.T, low).T)
        dv.append(dot(low, do_h))
        dp = dot(v_h, do_h.T)
        ds = (probs * (dp - jnp.sum(dp * probs, 0, keepdims=True))).astype(bf16)
        dq.append(dot(k_h.T, ds).T * factor)
        dk.append(dot(ds, q_h) * factor)
    mixed = jnp.concatenate(mixed, 1).astype(bf16)
    dq, dk, dv = (jnp.concatenate(v, 1) for v in (dq, dk, dv))
    mixed_all = lax.all_gather(mixed, "img", axis=1, tiled=True)
    output = (resid + dot(mixed_all, ko) + vec[8]).astype(bf16)

    dqkv = jnp.concatenate([dq, dk[tokens:], dv[tokens:]], 1).astype(bf16)
    dctx = jnp.concatenate([dk[:tokens], dv[:tokens]], 1)
    dn_part = lax.dot_general(dqkv, kq, (((1,), (1,)), ((), ())), preferred_element_type=f32)
    dn = lax.psum_scatter(dn_part.astype(bf16), "img", scatter_dimension=1, tiled=True).astype(f32)
    dy1 = dy_wide + group_back(dn * vec[6], normed3, inverse3, size)
    dh2 = dy1.astype(bf16)

    def turned(kernel):
        return kernel.reshape(9, chans, width).transpose(0, 2, 1).reshape(9 * width, chans)

    def conv_back(dh, kernel, act):
        field = taps_of(dh, rows, cols, True)
        part = dot(field, turned(kernel)).astype(bf16)
        grad = lax.psum_scatter(part, "img", scatter_dimension=1, tiled=True).astype(f32)
        kernel_grad = lax.dot_general(act, field, (((0,), (0,)), ((), ())), preferred_element_type=f32)
        return grad, kernel_grad.reshape(chans, 9, width).transpose(1, 0, 2).reshape(9 * chans, width)

    da2, gk2 = conv_back(dh2, k2, act2)
    du = da2 * silu_slope(pre2)
    dscale = jnp.sum(du * affine2, 0)
    dshift = jnp.sum(du, 0)
    dz = du * (1.0 + scale)
    dh1 = group_back(dz * vec[3], normed2, inverse2, size).astype(bf16)
    da1, gk1 = conv_back(dh1, k1, act1)
    dt1 = da1 * silu_slope(pre1)
    in_grad = (dy1 + group_back(dt1 * vec[0], normed1, inverse1, size)).astype(bf16)

    tops = lax.all_to_all(jnp.stack([output, in_grad]), "img", 1, 2, tiled=True)
    gkq = lax.dot_general(affine3, dqkv, (((0,), (0,)), ((), ())), preferred_element_type=f32)
    gkc = lax.dot_general(context[0], dctx.astype(bf16), (((0,), (0,)), ((), ())), preferred_element_type=f32)
    gko = lax.dot_general(mixed_all, dy, (((0,), (0,)), ((), ())), preferred_element_type=f32)
    gke = cond_act[0].astype(f32)[:, None] * jnp.concatenate([dscale, dshift])[None, :]
    grad_vec = jnp.stack(
        [
            jnp.sum(dt1 * normed1, 0),
            jnp.sum(dt1, 0),
            jnp.sum(dh1.astype(f32), 0),
            jnp.sum(dz * normed2, 0),
            jnp.sum(dz, 0),
            jnp.sum(dh2.astype(f32), 0),
            jnp.sum(dn * normed3, 0),
            jnp.sum(dn, 0),
            jnp.sum(dy_wide, 0),
        ]
        + [jnp.sum(v.astype(f32), 0) for v in jnp.split(dqkv, 3, 1)]
        + [jnp.sum(v, 0) for v in jnp.split(dctx, 2, 1)]
        + [dscale, dshift],
        0,
    )
    grads = (gk1, gk2, gkq, gkc, gke, gko)
    pieces = []
    for w, g in zip(shards, grads):
        wide = w.shape[1] // chans
        piece = g.reshape(count, w.shape[0], wide, width).transpose(0, 2, 1, 3)
        pieces.append(piece.reshape(count, wide * w.shape[0], width))
    packed = jnp.concatenate(pieces, 1).astype(bf16)
    packed = lax.psum_scatter(packed, "dp", scatter_dimension=0, tiled=True).astype(f32)
    packed = lax.all_to_all(packed.astype(bf16), "img", 0, 0, tiled=True).astype(f32)
    outs = []
    start = 0
    for w, length in zip(shards, lengths):
        wide = w.shape[1] // chans
        piece = packed[:, start : start + length].reshape(parts, wide, w.shape[0], width)
        outs.append(piece.transpose(2, 1, 0, 3).reshape(w.shape))
        start += length
    vec_sum = lax.all_gather(lax.psum(grad_vec, "dp"), "img", axis=1, tiled=True)
    each = chans // count
    g_vec = lax.dynamic_slice_in_dim(
        vec_sum, (lax.axis_index("dp") * parts + place) * each, each, 1
    )
    g1, g2, gq, gc, ge, go = outs
    return (tops[0].reshape(image.shape), tops[1].reshape(image.shape), g1, g2, ge, gq, gc, go, g_vec)


def solution(mesh):
    whole = P(("dp", "img"), None)
    field = P("dp", "img", None, None)
    in_specs = (
        field, P("dp", None), P("dp", None, None), whole, whole, whole, whole, whole, whole,
        P(None, ("dp", "img")), field,
    )
    out_specs = (field, field, whole, whole, whole, whole, whole, whole, P(None, ("dp", "img")))
    return jax.shard_map(
        on_device, mesh=mesh, in_specs=in_specs, out_specs=out_specs, check_vma=False
    )
```

time: 1510 us -> 491 us (0.33)
  waiting for transfers between devices: 1130 us -> 160 us
  matrix products: 130 us -> 47.8 us
  local copies, waits for them, and re-layouts: 59.4 us -> 113 us
  blocking collectives: 128 us -> 94.4 us
  other arithmetic: 21.3 us -> 38.9 us
    reduce_scatter x6 -> x1, waiting for transfers between devices: 695 us -> 78.9 us  [on_device(): lax.psum_scatter(packed, 'dp', scatter_dimension=0, tiled=True).astype(f32)]
    unnamed x16 -> x12, waiting for transfers between devices: 240 us -> 30.1 us
    all_gather x6 -> x5, waiting for transfers between devices: 184 us -> 38.1 us  [the longest x1 24.9 us: on_device(): packed = lax.all_gather(packed, 'dp', axis=0, tiled=True)]
    dot_general x71 -> x27, matrix products: 130 us -> 47.8 us  [the longest x20 30.6 us: dot(): return jnp.dot(a, b, preferred_element_type=f32)]
    all_gather x2 -> x3, blocking collectives: 82.9 us -> 54.3 us  [the longest x1 41.9 us: on_device(): lax.all_gather(vectors, ('dp', 'img'), axis=1, tiled=True).astype(f32)]
    psum x6 -> x1, blocking collectives: 45.3 us -> 20.4 us  [on_device(): lax.psum(grad_vec, 'dp')]
    all_to_all x0 -> x1, blocking collectives: none -> 19.7 us  [on_device(): packed = lax.all_to_all(packed, 'img', 0, 0, tiled=True)]
    reshape x0 -> x15, local copies, waits for them, and re-layouts: none -> 16.6 us  [the longest x6 4.69 us: columns(): weight.reshape(rows, chans // (parts * 128), parts, 128)]
  transfers between devices with their start and end apart: 22 -> 12, of which waited for: 18 -> 7; matrix products, arithmetic and copies ran while one was open for 5% -> 27% of each run, Pallas kernels for 0% -> 0%
where the time goes in v1:
time: 491 us; the launch traced here: 483 us
  waiting for transfers between devices  160 us (33%)
  local copies, waits for them, and re-layouts  113 us (23%)
  blocking collectives  94.4 us (19%)
  matrix products  47.8 us (10%)
  other arithmetic  38.9 us (8%)
  between operations  16 us (3%)
  starting transfers between devices  11.9 us (2%)
    reduce_scatter x1, waiting for transfers between devices, on_device(): lax.psum_scatter(packed, 'dp', scatter_dimension=0, tiled=True).astype(f32)  78.9 us
    all_gather x1, blocking collectives, on_device(): lax.all_gather(vectors, ('dp', 'img'), axis=1, tiled=True).astype(f32)  41.9 us
    unnamed x227, local copies, waits for them, and re-layouts  36.1 us
    dot_general x20, matrix products, dot(): return jnp.dot(a, b, preferred_element_type=f32)  30.6 us
    unnamed x12, waiting for transfers between devices  30.1 us
    all_gather x1, waiting for transfers between devices, on_device(): packed = lax.all_gather(packed, 'dp', axis=0, tiled=True)  24.9 us
    psum x1, blocking collectives, on_device(): lax.psum(grad_vec, 'dp')  20.4 us
    all_to_all x1, blocking collectives, on_device(): packed = lax.all_to_all(packed, 'img', 0, 0, tiled=True)  19.7 us
  transfers between devices with their start and end apart: 12, of which 7 were waited for; matrix products, arithmetic and copies ran while one was open for 27% of the time, Pallas kernels for 0%

profile of v1, /device:TPU:0, one launch (start us, length us, event | category | flops | bytes accessed | tf_op | source)
XLA Modules:
  0.0 482.7 jit_solution(3559549318462945113)
XLA Ops:
  13.3 19.7 %all_to_all.40 = bf16[4,608,128]{2,1,0:T(8,128)(2,1)} all-to-all(bf16[4,608,128]{2,1,0:T(8,128)(2,1)S(1)} %copy.125), channel_id=1, replica_groups=mesh['dp'=8,'img'=4] {'img'}, dimensions={0} | all-to-all | bytes 1245184 | tf_op jit(solution)/shard_map/all_to_all | solution.py:76
  33.1 41.9 %all_gather.25 = bf16[16,512]{0,1:T(8,128)(2,1)S(1)} all-gather(bf16[16,16]{0,1:T(8,128)(2,1)S(1)} %copy.117), channel_id=1, replica_groups=mesh['dp'=8,'img'=4] {'dp','img'}, dimensions={1}, use_global_device_ids=true | all-gather | bytes 16896 | tf_op jit(solution)/shard_map/all_gather | solution.py:86
  81.5 4.0 pad_slice_fusion.8
  95.4 24.9 %all-gather.8.cloned.1.call-done = bf16[32,608,128]{2,1,0:T(8,128)(2,1)} async-done(((bf16[4,608,128]{2,1,0:T(8,128)(2,1)}), bf16[32,608,128]{2,1,0:T(8,128)(2,1)}) %all-gather.8.cloned.1.call-update) | async-done | bytes 4980752 | tf_op jit(solution)/shard_map/all_gather | solution.py:77
  126.5 5.6 %fusion.91 = (f32[128]{0:T(128)S(1)}, f32[1024,128]{1,0:T(8,128)S(1)}) fusion(f32[128]{0:T(128)S(1)} %get-tuple-element.99, bf16[1024,4608]{1,0:T(8,128)(2,1)} %constant_dynamic-update-slice_fusion, bf16[4608,128]{1,0:T(8,128)(2,1)S(1)} %bitcast.279), kind=kOutput, calls=%fused_computation.279 | convolution fusion | flops 1208221568 | bytes 11142144 | tf_op jit(solution)/shard_map/dot_general | solution.py:16
  136.2 13.1 %all-gather.10.cloned.1.call-done = bf16[1024,512]{1,0:T(8,128)(2,1)} async-done(((bf16[1024,128]{1,0:T(8,128)(2,1)}), bf16[1024,512]{1,0:T(8,128)(2,1)}) %all-gather.10.cloned.1.call-update) | async-done | bytes 1048592 | tf_op jit(solution)/shard_map/all_gather | solution.py:105
  149.3 6.9 %pad_slice_fusion = (bf16[16,64,512]{2,1,0:T(8,128)(2,1)S(1)}, bf16[16,64,512]{2,1,0:T(8,128)(2,1)S(1)}, bf16[16,64,512]{2,1,0:T(8,128)(2,1)S(1)}, bf16[16,64,51...) fusion(bf16[16,64,512]{2,1,0:T(8,128)(2,1)} %bitcast.274), kind=kLoop, calls=%fused_computation.35 | loop fusion | bytes 9437184 | tf_op jit(solution)/shard_map/slice | solution.py:49
  159.2 3.7 fusion.92
  168.0 7.2 %all_gather.30 = bf16[512,512]{1,0:T(8,128)(2,1)S(1)} all-gather(bf16[512,128]{1,0:T(8,128)(2,1)S(1)} %bitcast.316), channel_id=1, replica_groups=mesh['dp'=8,'img'=4] {'img'}, dimensions={1}, use_global_device_ids=true | all-gather | bytes 655360 | tf_op jit(solution)/shard_map/all_gather | solution.py:114
  178.8 4.1 all-to-all-start.1
  187.4 4.4 all-to-all-done.1
  220.2 22.5 %reduce-scatter.13.cloned.1.call-done = bf16[128,1024]{1,0:T(8,128)(2,1)} async-done(((bf16[512,1024]{1,0:T(8,128)(2,1)}), bf16[128,1024]{1,0:T(8,128)(2,1)}) %reduce-scatter.13.cloned.1.call-update) | async-done | bytes 262160
  258.8 3.0 convolution_convert_fusion.6
  269.2 3.4 convolution_convert_fusion.9
  274.4 6.7 %reduce-scatter.15.cloned.1.call-done = bf16[128,1024]{1,0:T(8,128)(2,1)} async-done(((bf16[512,1024]{1,0:T(8,128)(2,1)}), bf16[128,1024]{1,0:T(8,128)(2,1)}) %reduce-scatter.15.cloned.1.call-update) | async-done | bytes 262160
  313.9 4.3 convolution_convert_fusion
  322.4 4.3 copy.137
  326.7 3.3 convolution_convert_fusion.2
  346.6 3.5 all-to-all-start.2
  350.0 8.8 %all-to-all-done.2 = bf16[2,1024,128]{2,0,1:T(2,128)(2,1)S(1)} async-done(((bf16[2,1024,128]{2,0,1:T(2,128)(2,1)}), bf16[2,1024,128]{2,0,1:T(2,128)(2,1)S(1)}, u32[]{:S(2)}, u32[]{:S(2)}) %all-to-all-start.2) | async-done | bytes 524320 | tf_op jit(solution)/shard_map/all_to_all | solution.py:172
  358.9 78.9 %reduce-scatter.11.cloned.1.call-done = bf16[4,608,128]{2,1,0:T(8,128)(2,1)} async-done(((bf16[32,608,128]{2,1,0:T(8,128)(2,1)}), bf16[4,608,128]{2,1,0:T(8,128)(2,1)}) %reduce-scatter.11.cloned.1.call-update) | async-done | bytes 622608 | tf_op jit(solution)/shard_map/reduce_scatter | solution.py:201
  437.8 3.5 all-to-all-start.3
  441.7 20.4 %psum.7 = f32[16,128]{1,0:T(8,128)S(1)} all-reduce(f32[16,128]{1,0:T(8,128)S(1)} %stack.87), channel_id=1, replica_groups=mesh['dp'=8,'img'=4] {'dp'}, use_global_device_ids=true, to_apply=%region_50.51 | all-reduce | flops 2048 | bytes 16384 | tf_op jit(solution)/shard_map/psum | solution.py:210
  462.1 5.2 %all_gather.31 = f32[16,512]{1,0:T(8,128)S(1)} all-gather(f32[16,128]{1,0:T(8,128)S(1)} %psum.7), channel_id=1, replica_groups=mesh['dp'=8,'img'=4] {'img'}, dimensions={1}, use_global_device_ids=true | all-gather | bytes 40960 | tf_op jit(solution)/shard_map/all_gather | solution.py:210
  (439 shorter events, 163.4 us)
Async XLA Ops:
  7.2 178.2 %copy-start = (bf16[1,81,2048]{2,1,0:T(8,128)(2,1)S(1)}, bf16[1,81,2048]{2,1,0:T(8,128)(2,1)}, u32[]{:S(2)}) copy-start(bf16[1,81,2048]{2,1,0:T(8,128)(2,1)} %param.13) | copy-start | bytes 995332
  7.2 67.9 %all-gather.6.cloned.1.call-start = ((), (), s32[]{:S(2)}) async-start(), calls=%async_computation.8 | async-start | bytes 1310720 | tf_op jit(solution)/shard_map/all_gather | solution.py:89
  7.9 112.4 %all-gather.8.cloned.1.call-start = ((), (), s32[]{:S(2)}) async-start(), calls=%async_computation.9 | async-start | bytes 5603328 | tf_op jit(solution)/shard_map/all_gather | solution.py:77
  33.0 116.4 %all-gather.10.cloned.1.call-start = ((), (), s32[]{:S(2)}) async-start(), calls=%async_computation.10 | async-start | bytes 1310720 | tf_op jit(solution)/shard_map/all_gather | solution.py:105
  134.1 61.8 %all-gather.12.cloned.1.call-start = ((), (), s32[]{:S(2)}) async-start(), calls=%async_computation.11 | async-start | bytes 1310720 | tf_op jit(solution)/shard_map/all_gather | solution.py:109
  178.8 13.0 %all-to-all-start.1 = ((bf16[2,256,512]{1,0,2:T(2,128)(2,1)}), bf16[2,256,512]{1,0,2:T(2,128)(2,1)}, u32[]{:S(2)}, u32[]{:S(2)}) async-start(bf16[2,256,512]{1,0,2:T(2,128)(2,1)} %copy.130), calls=%async_computation.1 | async-start | bytes 1048576 | tf_op jit(solution)/shard_map/all_to_all | solution.py:118
  183.0 59.8 %reduce-scatter.13.cloned.1.call-start = ((), (), s32[]{:S(2)}) async-start(), calls=%async_computation.14 | async-start | bytes 1310720
  217.7 63.4 %reduce-scatter.15.cloned.1.call-start = ((), (), s32[]{:S(2)}) async-start(), calls=%async_computation.15 | async-start | bytes 1310720
  256.1 80.1 %all-gather.14.cloned.1.call-start = ((), (), s32[]{:S(2)}) async-start(), calls=%async_computation.12 | async-start | bytes 1310720 | tf_op jit(solution)/shard_map/all_gather | solution.py:142
  274.4 65.9 %reduce-scatter.17.cloned.1.call-start = ((), (), s32[]{:S(2)}) async-start(), calls=%async_computation.16 | async-start | bytes 1310720
  305.3 132.4 %reduce-scatter.11.cloned.1.call-start = ((), (), s32[]{:S(2)}) async-start(), calls=%async_computation.13 | async-start | bytes 5603328 | tf_op jit(solution)/shard_map/reduce_scatter | solution.py:201
  345.0 96.4 %copy-start.25 = (bf16[1024,64]{0,1:T(8,128)(2,1)S(1)}, bf16[1024,64]{0,1:T(8,128)(2,1)}, u32[]{:S(2)}) copy-start(bf16[1024,64]{0,1:T(8,128)(2,1)} %copy-done.24) | copy-start | bytes 393220
  345.0 96.5 %copy-start.69 = (f32[128]{0:T(128)S(1)}, f32[128]{0:T(128)}, u32[]{:S(2)}) copy-start(f32[128]{0:T(128)} %get-tuple-element.11) | copy-start | bytes 1540
  345.1 96.5 %copy-start.70 = (f32[128]{0:T(128)S(1)}, f32[128]{0:T(128)}, u32[]{:S(2)}) copy-start(f32[128]{0:T(128)} %get-tuple-element.18) | copy-start | bytes 1540
  345.1 96.5 %copy-start.73 = (f32[128]{0:T(128)S(1)}, f32[128]{0:T(128)}, u32[]{:S(2)}) copy-start(f32[128]{0:T(128)} %get-tuple-element.27) | copy-start | bytes 1540
  345.1 96.5 %copy-start.74 = (f32[128]{0:T(128)S(1)}, f32[128]{0:T(128)}, u32[]{:S(2)}) copy-start(f32[128]{0:T(128)} %get-tuple-element.29) | copy-start | bytes 1540
  345.1 96.5 %copy-start.75 = (f32[128]{0:T(128)S(1)}, f32[128]{0:T(128)}, u32[]{:S(2)}) copy-start(f32[128]{0:T(128)} %get-tuple-element.31) | copy-start | bytes 1540
  345.1 96.5 %copy-start.76 = (f32[128]{0:T(128)S(1)}, f32[128]{0:T(128)}, u32[]{:S(2)}) copy-start(f32[128]{0:T(128)} %get-tuple-element.33) | copy-start | bytes 1540
  345.1 96.5 %copy-start.80 = (f32[128]{0:T(128)S(1)}, f32[128]{0:T(128)}, u32[]{:S(2)}) copy-start(f32[128]{0:T(128)} %get-tuple-element.14) | copy-start | bytes 1540
  345.1 96.5 %copy-start.81 = (f32[128]{0:T(128)S(1)}, f32[128]{0:T(128)}, u32[]{:S(2)}) copy-start(f32[128]{0:T(128)} %get-tuple-element.22) | copy-start | bytes 1540
  345.1 96.5 %copy-start.82 = (f32[128]{0:T(128)S(1)}, f32[128]{0:T(128)}, u32[]{:S(2)}) copy-start(f32[128]{0:T(128)} %get-tuple-element.23) | copy-start | bytes 1540
  345.1 96.5 %copy-start.83 = (f32[128]{0:T(128)S(1)}, f32[128]{0:T(128)}, u32[]{:S(2)}) copy-start(f32[128]{0:T(128)} %get-tuple-element.25) | copy-start | bytes 1540
  346.6 12.3 %all-to-all-start.2 = ((bf16[2,1024,128]{2,0,1:T(2,128)(2,1)}), bf16[2,1024,128]{2,0,1:T(2,128)(2,1)S(1)}, u32[]{:S(2)}, u32[]{:S(2)}) async-start(bf16[2,1024,128]{2,0,1:T(2,128)(2,1)} %copy.134), calls=%async_computation.2 | async-start | bytes 1048576 | tf_op jit(solution)/shard_map/all_to_all | solution.py:172
  437.8 33.3 %all-to-all-start.3 = ((bf16[4,608,128]{2,1,0:T(8,128)(2,1)}), bf16[4,608,128]{2,1,0:T(8,128)(2,1)S(1)}, u32[]{:S(2)}, u32[]{:S(2)}) async-start(bf16[4,608,128]{2,1,0:T(8,128)(2,1)} %reduce-scatter.11.cloned.1.call-done), calls=%async_computation.4 | async-start | bytes 1245184 | tf_op jit(solution)/shard_map/all_to_all | solution.py:202
  (78 other events, 713.6 us)
Sparse Core Ops, SparseCore 0:
  9.6 24.6 all-gather.5
  36.4 83.8 all-gather.7
  134.2 15.1 all-gather.9
  164.7 16.8 all-gather.11
  217.9 24.8 reduce-scatter.12
  256.2 24.8 reduce-scatter.14
  283.3 16.7 all-gather.13
  305.5 24.9 reduce-scatter.16
  338.7 98.9 reduce-scatter.10

commit v2 on v1

--- a/solution.py
+++ b/solution.py
@@ -1,6 +1,11 @@
+import functools
+import types
+
 import jax
 import jax.numpy as jnp
 from jax import lax
+from jax.experimental import pallas as pl
+from jax.experimental.pallas import tpu as pltpu
 from jax.sharding import PartitionSpec as P
 
 HEADS = 8
@@ -53,6 +58,779 @@
 def columns(weight, parts):
     rows, chans = weight.shape
     return weight.reshape(rows, chans // (parts * 128), parts, 128).transpose(2, 1, 0, 3).reshape(parts, -1, 128)
+
+
+class Wires:
+    def __init__(self, sent, landed):
+        self.sent, self.landed, self.copies = sent, landed, []
+
+    def send(self, source, target, device):
+        at = len(self.copies)
+        copy = pltpu.make_async_remote_copy(
+            src_ref=source, dst_ref=target, send_sem=self.sent.at[at], recv_sem=self.landed.at[at],
+            device_id=device, device_id_type=pl.DeviceIdType.MESH,
+        )
+        copy.start()
+        self.copies.append(copy)
+        return copy
+
+    def drain(self):
+        for copy in self.copies:
+            copy.wait_send()
+
+
+def scratch_plan(g):
+    P, Q, C, B, N, J, X = g.P, g.Q, g.C, g.B, g.N, g.J, g.X
+    plan = dict(
+        X=((J, Q, C), bf16), vown=((16, C), bf16), vs1=((J, 16, C), bf16),
+        vsum=((16, C), bf16), vs2=((N, 16, C), bf16), vecs=((J, 16, B), f32),
+        eall=((N, 1, g.E), f32), wemb=((2 * g.RE, 2 * C), bf16), epart=((N, 1, 2 * C), f32),
+        erx=((N, 1, 2 * C), f32), esum=((J, 1, 2 * C), f32), emb=((1, 2 * C), f32),
+        A1=((2, P + 2 * g.COLS, 2 * B), bf16), A2=((2, P + 2 * g.COLS, 2 * B), bf16),
+        N3=((2, P, 2 * B), bf16), O=((2, P, 2 * B), bf16),
+        A1T=((C, P), bf16), A2T=((C, P), bf16), N3T=((C, P), bf16), OT=((C, P), bf16),
+        st1=((J, 8, B), f32), xj=((P, B), bf16),
+        h1=((P, B), f32), y1=((P, B), f32), dy1=((P, B), f32), tmp=((P, B), f32),
+        W1T=((2, 9 * B, 2 * B), bf16), W2T=((2, 9 * B, 2 * B), bf16), WqT=((2, 3 * B, 2 * B), bf16),
+        ctx=((B, X), bf16), ctxT=((X, B), bf16),
+        Kb=((P + B, B), bf16), Vb=((P + B, B), bf16), KT=((B, P + B), bf16), VT=((B, P + B), bf16),
+        qs=((P, B), bf16), dK=((P + B, B), f32), dV=((P + B, B), f32), dqkv=((3, P, B), bf16),
+        WoF=((2, C, 2 * B), bf16), dopx=((Q, C), bf16), doj=((P, B), bf16), dyj=((P, B), bf16),
+        outj=((P, B), bf16), inj=((P, B), bf16),
+        S=((3, P + 2 * g.COLS, B), bf16),
+        dse=((J, 2, B), f32), dsall=((N, J, 2, B), f32), geb=((2 * g.RE, 2 * C), f32),
+        gvec=((16, B), f32), gvs=((N, 16, B), f32), gvi=((J, 16, B), f32), gvt=((16, B), f32),
+    )
+    half = dict(ps=((2, 2, P, B), bf16), rc=((2, P, B), bf16), sy=((P, B), bf16), ry=((P, B), bf16))
+    groups = [plan, half, half, half]
+    for wide, rows in g.weights:
+        depth = rows * J
+        groups.append(dict(
+            w=((wide, depth * N, B), bf16), g=((wide, depth * N, B), bf16),
+            rx=((N // 2, wide, depth, B), bf16), zs=((N // 2, wide, depth, B), bf16),
+            zr=((N // 2, wide, depth, B), bf16), fin=((wide, depth, B), bf16), gr=((J, wide, rows, B), bf16),
+        ))
+    return groups
+
+
+def body(g, groups, *refs):
+    (x_in, cond, ctx_in, w1, w2, w_emb, w_q, w_c, w_o, vec_in, dy_in) = refs[:11]
+    (out, in_grad, gc1, gc2, g_emb, g_q, g_c, g_o, g_v) = refs[11:20]
+    left = list(refs[20:-2])
+    spaces = [types.SimpleNamespace(**{name: left.pop(0) for name in group}) for group in groups]
+    s, dn_bufs, da2_bufs, da1_bufs = spaces[:4]
+    c1, c2, wq, wc, wo = spaces[4:]
+    for weight, shape, ref in zip(spaces[4:], g.weights, (w1, w2, w_q, w_c, w_o)):
+        weight.wide, weight.rows, weight.ref = shape[0], shape[1], ref
+        weight.depth = weight.rows * g.J
+    rest = (wq, wc, wo)
+    P, Q, C, B, N, J, COLS, SIZE = g.P, g.Q, g.C, g.B, g.N, g.J, g.COLS, g.SIZE
+    T, E, RE = g.T, g.E, g.RE
+    Z = N // 2
+    STEPS = P // Q
+    wires = Wires(refs[-2], refs[-1])
+    send = wires.send
+    d = lax.axis_index("dp")
+    j = lax.axis_index("img")
+    flat = d * J + j
+    z, xx = lax.div(d, 2), lax.rem(d, 2)
+    yy, cc = lax.div(j, 2), lax.rem(j, 2)
+    sib = (d, yy * 2 + (1 - cc))
+    ypeer = (d, (1 - yy) * 2 + cc)
+    diag = (d, (1 - yy) * 2 + (1 - cc))
+    img_peers = [ypeer, diag, sib]
+    dp_peers = [(lax.rem(d + k, N), j) for k in range(1, N)]
+    zdev = [lax.rem(z + k, Z) for k in range(Z)]
+    zsrc = [lax.rem(z + Z - k, Z) for k in range(Z)]
+    xpeer = (z * 2 + (1 - xx), j)
+
+    def lanes(k):
+        return pl.ds(pl.multiple_of(k * B, B), B)
+
+    def rows_at(start, size, unit):
+        return pl.ds(pl.multiple_of(start, unit), size)
+
+    def px(i):
+        return pl.ds(pl.multiple_of(i * Q, Q), Q)
+
+    def each(fn, init=None):
+        if init is None:
+            lax.fori_loop(0, STEPS, lambda i, carry: (fn(i), carry)[1], 0)
+            return None
+        return lax.fori_loop(0, STEPS, fn, init)
+
+    def mm(a, b):
+        return jnp.dot(a, b, preferred_element_type=f32)
+
+    def mm_t(a, b):
+        return lax.dot_general(a, b, (((1,), (1,)), ((), ())), preferred_element_type=f32)
+
+    lane8 = lax.broadcasted_iota(jnp.int32, (8, B), 1)
+
+    def group_sum(row):
+        v = jnp.broadcast_to(row, (8, B))
+        step = 1
+        while step < SIZE:
+            down, up = pltpu.roll(v, B - step, 1), pltpu.roll(v, step, 1)
+            v = v + jnp.where((lane8 & step) == 0, down, up)
+            step *= 2
+        return v[0:1]
+
+    def colsum(v):
+        return jnp.sum(v, axis=0, keepdims=True)
+
+    zero_row = jnp.zeros((1, B), f32)
+    count = P * SIZE
+
+    def moments(load):
+        total = each(lambda i, a: a + colsum(load(i)), zero_row)
+        mean = group_sum(total) * (1.0 / count)
+        spread = each(lambda i, a: a + colsum(jnp.square(load(i) - mean)), zero_row)
+        return mean, lax.rsqrt(group_sum(spread) * (1.0 / count) + 1e-05)
+
+    col = lax.rem(lax.broadcasted_iota(jnp.int32, (Q, B), 0), COLS)
+
+    def from_left(v):
+        return jnp.where(col == 0, 0.0, pltpu.roll(v, 1, 0))
+
+    def from_right(v):
+        return jnp.where(col == COLS - 1, 0.0, pltpu.roll(v, Q - 1, 0))
+
+    hot = lax.broadcasted_iota(jnp.int32, (16, C), 1) == (
+        lax.broadcasted_iota(jnp.int32, (16, C), 0) + flat * g.VW
+    )
+    hot = jnp.where(hot, 1.0, 0.0).astype(bf16)
+    own_vec = mm(vec_in[...], hot).astype(bf16)
+    s.vown[...] = own_vec
+    s.vs1[j] = own_vec
+    e_own = cond[...].astype(f32)
+    e_own = (e_own * jax.nn.sigmoid(e_own)).astype(bf16).astype(f32)
+    s.eall[d] = e_own
+
+    barrier = pltpu.get_barrier_semaphore()
+    for device in img_peers + dp_peers:
+        pl.semaphore_signal(barrier, inc=1, device_id=device, device_id_type=pl.DeviceIdType.MESH)
+    pl.semaphore_wait(barrier, len(img_peers) + len(dp_peers))
+
+    def stage_img(W):
+        start = d * W.depth + j * W.rows
+        W.img = []
+        for device in img_peers:
+            for t in range(W.wide):
+                source = W.ref.at[:, rows_at(t * C + device[1] * B, B, B)]
+                W.img.append(send(source, W.w.at[t, rows_at(start, W.rows, 16), :], device))
+
+    def own_img(W):
+        start = d * W.depth + j * W.rows
+        for t in range(W.wide):
+            W.w[t, rows_at(start, W.rows, 16), :] = W.ref[:, rows_at(t * C + j * B, B, B)]
+
+    def block(W, ref, owner):
+        return ref.at[:, rows_at(owner * W.depth, W.depth, 16), :]
+
+    def stage_z(W):
+        for copy in W.img:
+            copy.wait_recv()
+        mine = block(W, W.w, d)
+        W.z = [send(mine, mine, (zdev[k] * 2 + xx, j)) for k in range(1, Z)]
+        W.x = [send(mine, mine, xpeer)]
+
+    def forward(W):
+        for k, copy in enumerate(W.z, 1):
+            copy.wait_recv()
+            here = block(W, W.w, zsrc[k] * 2 + xx)
+            W.x.append(send(here, here, xpeer))
+
+    def arrive(W):
+        for copy in W.x:
+            copy.wait_recv()
+
+    def gather_start(mine):
+        return types.SimpleNamespace(y=send(mine, mine, ypeer), c=send(mine, mine, sib))
+
+    def gather_near(state):
+        state.c.wait_recv()
+
+    def gather_far(state, theirs):
+        state.y.wait_recv()
+        state.f = send(theirs, theirs, sib)
+
+    def gather_end(state):
+        state.f.wait_recv()
+
+    stage_img(c1)
+    v_stage1 = [send(s.vown, s.vs1.at[j], device) for device in img_peers]
+    x_own = s.X.at[j]
+    x_state = types.SimpleNamespace(y=send(x_in, x_own, ypeer), c=send(x_in, x_own, sib))
+    e_stage1 = [send(s.eall.at[d], s.eall.at[d], device) for device in dp_peers]
+    own_img(c1)
+    s.X[j] = x_in[...]
+    for W in (c2, *rest):
+        own_img(W)
+    for buf in (s.A1, s.A2):
+        for h in range(2):
+            buf[h, 0:COLS, :] = jnp.zeros((COLS, 2 * B), bf16)
+            buf[h, P + COLS : P + 2 * COLS, :] = jnp.zeros((COLS, 2 * B), bf16)
+    for c in range(3):
+        s.S[c, 0:COLS, :] = jnp.zeros((COLS, B), bf16)
+        s.S[c, P + COLS : P + 2 * COLS, :] = jnp.zeros((COLS, B), bf16)
+    s.ctx[...] = jnp.zeros((B, g.X), bf16)
+    s.ctx[0:T, :] = ctx_in[...]
+    stage_z(c1)
+    for copy in v_stage1:
+        copy.wait_recv()
+    total = s.vs1[0].astype(f32)
+    for k in range(1, J):
+        total = total + s.vs1[k].astype(f32)
+    s.vsum[...] = total.astype(bf16)
+    s.vs2[d] = total.astype(bf16)
+    v_stage2 = [send(s.vsum, s.vs2.at[d], device) for device in dp_peers]
+
+    x_state.y.wait_recv()
+    far = s.X.at[(1 - yy) * 2 + cc]
+    x_state.f = send(far, far, sib)
+    for W in (c2, *rest):
+        stage_img(W)
+    dy_copies = [
+        send(dy_in.at[:, lanes(device[1])], s.dyj.at[rows_at(j * Q, Q, Q), :], device) for device in img_peers
+    ]
+    s.dyj[rows_at(j * Q, Q, Q), :] = dy_in[:, lanes(j)]
+
+    for copy in e_stage1:
+        copy.wait_recv()
+    s.wemb[...] = jnp.zeros((2 * RE, 2 * C), bf16)
+    s.wemb[rows_at(lax.rem(flat, 2) * RE, RE, 16), :] = w_emb[...]
+    e_at = rows_at(lax.div(flat, 2) * (2 * RE), 2 * RE, B)
+    e_rows = jnp.concatenate([s.eall[k, :, e_at] for k in range(N)], axis=0)
+    part = mm(e_rows.astype(bf16), s.wemb[...])
+    for k in range(N):
+        s.epart[k] = part[k : k + 1]
+    s.erx[d] = s.epart[d]
+    e_stage2 = [send(s.epart.at[device[0]], s.erx.at[d], device) for device in dp_peers]
+
+    x_state.c.wait_recv()
+    x_state.f.wait_recv()
+
+    def load_x(k):
+        return lambda i: s.X[i, :, k * B : (k + 1) * B].astype(f32)
+
+    for k in range(J):
+        mean, inverse = moments(load_x(k))
+        s.st1[k, 0:1, :] = mean
+        s.st1[k, 1:2, :] = inverse
+    for copy in e_stage2:
+        copy.wait_recv()
+    total = s.erx[0]
+    for k in range(1, N):
+        total = total + s.erx[k]
+    s.esum[j] = total
+    e_stage3 = [send(s.esum.at[j], s.esum.at[j], device) for device in img_peers]
+    for copy in v_stage2:
+        copy.wait_recv()
+    total = s.vs2[0].astype(f32)
+    for k in range(1, N):
+        total = total + s.vs2[k].astype(f32)
+    for k in range(J):
+        s.vecs[k] = total[:, k * B : (k + 1) * B]
+
+    def vec(row):
+        return s.vecs[j, row : row + 1, :]
+
+    forward(c1)
+    for k in range(J):
+        mean, inverse = s.st1[k, 0:1, :], s.st1[k, 1:2, :]
+        gain, bias = s.vecs[k, 0:1, :], s.vecs[k, 1:2, :]
+        load = load_x(k)
+
+        def act(i):
+            t1 = (load(i) - mean) * inverse * gain + bias
+            a1 = t1 * jax.nn.sigmoid(t1)
+            s.A1[k // 2, rows_at(i * Q + COLS, Q, COLS), (k % 2) * B : (k % 2 + 1) * B] = a1.astype(bf16)
+
+        each(act)
+
+    def turn(source, target, offset):
+        def one(i):
+            for h in range(2):
+                v = source[h, rows_at(i * Q + offset, Q, 16), :]
+                target[h * 2 * B : (h + 1) * 2 * B, px(i)] = v.T
+        each(one)
+
+    each(lambda i: s.xj.__setitem__((px(i), slice(None)), s.X[i, :, lanes(j)]))
+    turn(s.A1, s.A1T, COLS)
+    for copy in e_stage3:
+        copy.wait_recv()
+    total = s.esum[0]
+    for k in range(1, J):
+        total = total + s.esum[k]
+    s.emb[...] = total
+    scale = 1.0 + (s.emb[:, lanes(j)] + vec(14))
+    shift = s.emb[:, lanes(j + J)] + vec(15)
+    stage_z(c2)
+    arrive(c1)
+
+    def convolve(A, W, emit):
+        def one(i):
+            left = jnp.concatenate(
+                [A[h, rows_at(i * Q + r * COLS, Q, COLS), :] for r in range(3) for h in range(2)], axis=1
+            )
+            right = jnp.concatenate(
+                [
+                    jnp.concatenate([W[0, (3 * r + c) * C : (3 * r + c + 1) * C, :] for r in range(3)], axis=0)
+                    for c in range(3)
+                ],
+                axis=1,
+            )
+            p = mm(left, right)
+            emit(i, p[:, B : 2 * B] + from_left(p[:, :B]) + from_right(p[:, 2 * B :]))
+        each(one)
+
+    def save_h1(i, v):
+        s.h1[px(i), :] = v + vec(2)
+
+    convolve(s.A1, c1.w, save_h1)
+    mean2, inv2 = moments(lambda i: s.h1[px(i), :])
+
+    def xh2(i):
+        return (s.h1[px(i), :] - mean2) * inv2
+
+    def u_of(i):
+        return (xh2(i) * vec(3) + vec(4)) * scale + shift
+
+    def act2(i):
+        u = u_of(i)
+        s.A2[yy, rows_at(i * Q + COLS, Q, COLS), lanes(cc)] = (u * jax.nn.sigmoid(u)).astype(bf16)
+
+    each(act2)
+    inside = pl.ds(COLS, P)
+    a2_state = gather_start(s.A2.at[yy, inside, lanes(cc)])
+    forward(c2)
+    for W in rest:
+        stage_z(W)
+    gather_far(a2_state, s.A2.at[1 - yy, inside, lanes(cc)])
+    gather_near(a2_state)
+    gather_end(a2_state)
+    arrive(c2)
+
+    def save_y1(i, v):
+        s.y1[px(i), :] = s.xj[px(i), :].astype(f32) + v + vec(5)
+
+    convolve(s.A2, c2.w, save_y1)
+    mean3, inv3 = moments(lambda i: s.y1[px(i), :])
+
+    def xh3(i):
+        return (s.y1[px(i), :] - mean3) * inv3
+
+    def act3(i):
+        s.N3[yy, px(i), lanes(cc)] = (xh3(i) * vec(6) + vec(7)).astype(bf16)
+
+    each(act3)
+    n_state = gather_start(s.N3.at[yy, :, lanes(cc)])
+    for W in rest:
+        forward(W)
+    turn(s.A2, s.A2T, COLS)
+
+    def turn_weights(W, target, taps, stride):
+        for h in range(2):
+            for t in range(taps):
+                v = W(t)[rows_at(h * 2 * B, 2 * B, 16), :]
+                target[h, t * B : (t + 1) * B, :] = v.T
+
+    def conv_tap(W):
+        return lambda t: W.w.at[0, pl.ds(t * C, C), :]
+
+    turn_weights(conv_tap(c2), s.W2T, 9, C)
+    gather_far(n_state, s.N3.at[1 - yy, :, lanes(cc)])
+    turn_weights(conv_tap(c1), s.W1T, 9, C)
+    s.ctxT[...] = s.ctx[...].T
+    for W in rest:
+        arrive(W)
+    wo_at = s.WoF.at[yy, :, lanes(cc)]
+    s.WoF[yy, :, lanes(cc)] = wo.w[0]
+    wo_state = gather_start(wo_at)
+    turn_weights(lambda t: wq.w.at[t], s.WqT, 3, C)
+    tokens = lax.broadcasted_iota(jnp.int32, (B, B), 0) < T
+    for t, target in enumerate((s.Kb, s.Vb)):
+        v = mm(s.ctx[...], wc.w[t]) + vec(12 + t)
+        target[P : P + B, :] = jnp.where(tokens, v, 0.0).astype(bf16)
+    gather_far(wo_state, s.WoF.at[1 - yy, :, lanes(cc)])
+    gather_near(wo_state)
+    gather_end(wo_state)
+    for h in range(2):
+        part = mm_t(dy_in[:, 0 : 2 * B], s.WoF[0, h * 2 * B : (h + 1) * 2 * B, :])
+        part = part + mm_t(dy_in[:, 2 * B : 4 * B], s.WoF[1, h * 2 * B : (h + 1) * 2 * B, :])
+        s.dopx[:, h * 2 * B : (h + 1) * 2 * B] = part.astype(bf16)
+    do_copies = [
+        send(s.dopx.at[:, lanes(device[1])], s.doj.at[rows_at(j * Q, Q, Q), :], device)
+        for device in img_peers
+    ]
+    s.doj[rows_at(j * Q, Q, Q), :] = s.dopx[:, lanes(j)]
+    gather_near(n_state)
+    gather_end(n_state)
+
+    def project(i):
+        left = jnp.concatenate([s.N3[0, px(i), :], s.N3[1, px(i), :]], axis=1)
+        right = jnp.concatenate([wq.w[t] for t in range(3)], axis=1)
+        v = mm(left, right)
+        q = (v[:, :B] + vec(9)).astype(bf16)
+        s.qs[px(i), :] = (q.astype(f32) * g.FACTOR).astype(bf16)
+        s.Kb[px(i), :] = (v[:, B : 2 * B] + vec(10)).astype(bf16)
+        s.Vb[px(i), :] = (v[:, 2 * B :] + vec(11)).astype(bf16)
+
+    each(project)
+    for source, target in ((s.Kb, s.KT), (s.Vb, s.VT)):
+        for k in range(0, P + B, B):
+            target[:, k : k + B] = source[k : k + B, :].T
+    for copy in do_copies + dy_copies:
+        copy.wait_recv()
+    s.dK[...] = jnp.zeros((P + B, B), f32)
+    s.dV[...] = jnp.zeros((P + B, B), f32)
+
+    HEAD_ = g.HEAD
+    lane_row = lax.broadcasted_iota(jnp.int32, (1, B), 1)
+    known = lax.broadcasted_iota(jnp.int32, (B, Q), 0) < T
+
+    def attend(i):
+        q_i, do_i = s.qs[px(i), :], s.doj[px(i), :]
+        q_m, do_m, low, slope, mixed, back = [], [], [], [], [], []
+        for h in range(B // HEAD_):
+            keep = jnp.where(lax.div(lane_row, HEAD_) == h, 1.0, 0.0).astype(bf16)
+            qm, dom = q_i * keep, do_i * keep
+            scores = mm_t(s.Kb[...], qm)
+            scores = jnp.concatenate([scores[:P], jnp.where(known, scores[P:], -1e30)], axis=0)
+            top = jnp.max(scores, axis=0, keepdims=True)
+            e = jnp.exp(scores - top)
+            probs = e * (1.0 / jnp.sum(e, axis=0, keepdims=True))
+            pb = probs.astype(bf16)
+            mixed.append(mm(s.VT[h * HEAD_ : (h + 1) * HEAD_, :], pb))
+            dp = mm_t(s.Vb[...], dom)
+            inner = jnp.sum(dp * probs, axis=0, keepdims=True)
+            ds = (probs * (dp - inner)).astype(bf16)
+            back.append(mm(s.KT[h * HEAD_ : (h + 1) * HEAD_, :], ds))
+            q_m.append(qm)
+            do_m.append(dom)
+            low.append(pb)
+            slope.append(ds)
+        s.dV[...] += mm(jnp.concatenate(low, axis=1), jnp.concatenate(do_m, axis=0))
+        s.dK[...] += mm(jnp.concatenate(slope, axis=1), jnp.concatenate(q_m, axis=0))
+        s.O[yy, px(i), lanes(cc)] = jnp.concatenate(mixed, axis=0).T.astype(bf16)
+        s.dqkv[0, px(i), :] = (jnp.concatenate(back, axis=0).T * g.FACTOR).astype(bf16)
+
+    each(attend)
+    o_state = gather_start(s.O.at[yy, :, lanes(cc)])
+
+    def grads_kv(i):
+        s.dqkv[1, px(i), :] = s.dK[px(i), :].astype(bf16)
+        s.dqkv[2, px(i), :] = s.dV[px(i), :].astype(bf16)
+
+    each(grads_kv)
+
+    def scatter(bufs, left, right):
+        ps, rc, sy, ry = bufs.ps, bufs.rc, bufs.sy, bufs.ry
+        near = []
+        for slot in range(2):
+            half = 1 - yy if slot == 0 else yy
+
+            def one(i):
+                v = mm(left(i), right[half]).astype(bf16)
+                ps[slot, 0, px(i), :] = v[:, :B]
+                ps[slot, 1, px(i), :] = v[:, B:]
+
+            each(one)
+            near.append(send(ps.at[slot, 1 - cc], rc.at[slot], sib))
+            if slot == 0:
+                near[0].wait_recv()
+
+                def add(i):
+                    v = ps[0, cc, px(i), :].astype(f32) + rc[0, px(i), :].astype(f32)
+                    sy[px(i), :] = v.astype(bf16)
+
+                each(add)
+                across = send(sy, ry, ypeer)
+
+        def done():
+            near[1].wait_recv()
+            across.wait_recv()
+
+        def load(i):
+            v = ps[1, cc, px(i), :].astype(f32) + rc[1, px(i), :].astype(f32)
+            return v + ry[px(i), :].astype(f32)
+
+        return done, load
+
+    order = list(range(1, Z)) + [0]
+
+    def sum_start(W):
+        W.sx = {}
+        for k in order:
+            W.sx[k] = send(block(W, W.g, zdev[k] * 2 + (1 - xx)), W.rx.at[k], xpeer)
+
+    def sum_z(W):
+        W.sz = {}
+        for k in order:
+            W.sx[k].wait_recv()
+            at = rows_at((zdev[k] * 2 + xx) * W.depth, W.depth, 16)
+            v = W.g[:, at, :].astype(f32) + W.rx[k].astype(f32)
+            W.zs[k] = v.astype(bf16)
+            if k:
+                W.sz[k] = send(W.zs.at[k], W.zr.at[k], (zdev[k] * 2 + xx, j))
+
+    def sum_img(W):
+        v = W.zs[0].astype(f32)
+        for k in range(1, Z):
+            W.sz[k].wait_recv()
+            v = v + W.zr[k].astype(f32)
+        W.fin[...] = v.astype(bf16)
+        W.simg = [
+            send(W.fin.at[:, rows_at(device[1] * W.rows, W.rows, 16), :], W.gr.at[j], device)
+            for device in img_peers
+        ]
+        W.gr[j] = W.fin[:, rows_at(j * W.rows, W.rows, 16), :]
+
+    def sum_end(W, target):
+        for copy in W.simg:
+            copy.wait_recv()
+        for k in range(J):
+            for t in range(W.wide):
+                target[:, t * C + k * B : t * C + (k + 1) * B] = W.gr[k, t].astype(f32)
+
+    dn_done, dn_at = scatter(
+        dn_bufs, lambda i: jnp.concatenate([s.dqkv[t, px(i), :] for t in range(3)], axis=1), s.WqT
+    )
+    turn(s.N3, s.N3T, 0)
+    for h in range(2):
+        at = slice(h * 2 * B, (h + 1) * 2 * B)
+        v = mm(s.N3T[at, :], jnp.concatenate([s.dqkv[t] for t in range(3)], axis=1)).astype(bf16)
+        for t in range(3):
+            wq.g[t, at, :] = v[:, t * B : (t + 1) * B]
+    sum_start(wq)
+    d_ctx = jnp.concatenate([s.dK[P : P + B, :], s.dV[P : P + B, :]], axis=1).astype(bf16)
+    X_ = g.X
+    for k in range(0, X_, C):
+        v = mm(s.ctxT[k : k + C, :], d_ctx).astype(bf16)
+        wc.g[0, k : k + C, :] = v[:, :B]
+        wc.g[1, k : k + C, :] = v[:, B:]
+    sum_start(wc)
+    gather_far(o_state, s.O.at[1 - yy, :, lanes(cc)])
+    gather_near(o_state)
+    gather_end(o_state)
+
+    def finish(i):
+        left = jnp.concatenate([s.O[0, px(i), :], s.O[1, px(i), :]], axis=1)
+        s.outj[px(i), :] = (s.y1[px(i), :] + mm(left, wo.w[0]) + vec(8)).astype(bf16)
+
+    each(finish)
+
+    def to_pixels(source, target):
+        copies = [
+            send(source.at[rows_at(device[1] * Q, Q, Q), :], target.at[:, lanes(j)], device) for device in img_peers
+        ]
+        target[:, lanes(j)] = source[rows_at(j * Q, Q, Q), :]
+        return copies
+
+    out_copies = to_pixels(s.outj, out)
+    turn(s.O, s.OT, 0)
+    for h in range(2):
+        at = slice(h * 2 * B, (h + 1) * 2 * B)
+        wo.g[0, at, :] = mm(s.OT[at, :], s.dyj[...]).astype(bf16)
+    sum_start(wo)
+
+    def back_sums(grad, normed, factor):
+        def one(i, carry):
+            v = grad(i)
+            return carry[0] + colsum(v), carry[1] + colsum(v * normed(i))
+        first, second = each(one, (zero_row, zero_row))
+        return first, second, group_sum(first * factor) * (1.0 / count), group_sum(second * factor) * (1.0 / count)
+
+    dn_done()
+    dn_sum, dn_hat, m1, m2 = back_sums(dn_at, xh3, vec(6))
+
+    def shifted(i, v):
+        at = rows_at(i * Q + COLS, Q, COLS)
+        s.S[0, at, :] = from_right(v).astype(bf16)
+        s.S[1, at, :] = v.astype(bf16)
+        s.S[2, at, :] = from_left(v).astype(bf16)
+
+    def make_dh2(i, carry):
+        dy = s.dyj[px(i), :].astype(f32)
+        v = dy + (dn_at(i) * vec(6) - m1 - xh3(i) * m2) * inv3
+        s.dy1[px(i), :] = v
+        low = v.astype(bf16).astype(f32)
+        shifted(i, low)
+        return carry[0] + colsum(low), carry[1] + colsum(dy)
+
+    dh2_sum, dy_sum = each(make_dh2, (zero_row, zero_row))
+
+    def tap(t, start, size):
+        r, c = t // 3, t % 3
+        return s.S[c, rows_at(start + (2 - r) * COLS, size, COLS), :]
+
+    def field(i):
+        return jnp.concatenate([tap(t, i * Q, Q) for t in range(9)], axis=1)
+
+    def kernel_grad(W, turned):
+        for h in range(2):
+            at = slice(h * 2 * B, (h + 1) * 2 * B)
+            v = mm(turned[at, :], jnp.concatenate([tap(t, 0, P) for t in range(9)], axis=1)).astype(bf16)
+            for t in range(9):
+                W.g[0, t * C + h * 2 * B : t * C + (h + 1) * 2 * B, :] = v[:, t * B : (t + 1) * B]
+
+    da2_done, da2_at = scatter(da2_bufs, field, s.W2T)
+    kernel_grad(c2, s.A2T)
+    sum_z(wq)
+    sum_z(wc)
+    sum_z(wo)
+    sum_start(c2)
+    da2_done()
+
+    def slope_of(v):
+        sigma = jax.nn.sigmoid(v)
+        return sigma * (1.0 + v * (1.0 - sigma))
+
+    def make_du(i, carry):
+        du = da2_at(i) * slope_of(u_of(i))
+        s.tmp[px(i), :] = du
+        return carry[0] + colsum(du), carry[1] + colsum(du * xh2(i))
+
+    du_sum, du_hat = each(make_du, (zero_row, zero_row))
+    gain2 = scale * vec(3)
+    m1b = group_sum(du_sum * gain2) * (1.0 / count)
+    m2b = group_sum(du_hat * gain2) * (1.0 / count)
+
+    def make_dh1(i, carry):
+        v = (s.tmp[px(i), :] * gain2 - m1b - xh2(i) * m2b) * inv2
+        low = v.astype(bf16).astype(f32)
+        shifted(i, low)
+        return carry + colsum(low)
+
+    dh1_sum = each(make_dh1, zero_row)
+    dscale = vec(3) * du_hat + vec(4) * du_sum
+    da1_done, da1_at = scatter(da1_bufs, field, s.W1T)
+    kernel_grad(c1, s.A1T)
+    sum_start(c1)
+    s.dse[j] = jnp.concatenate([dscale, du_sum], axis=0)
+    ds_copies = [send(s.dse.at[j], s.dse.at[j], device) for device in img_peers]
+    for W in rest:
+        sum_img(W)
+    sum_z(c2)
+    for copy in ds_copies:
+        copy.wait_recv()
+    s.dsall[d] = s.dse[...]
+    ds_copies = [send(s.dse, s.dsall.at[d], device) for device in dp_peers]
+    da1_done()
+    mean1, inv1 = s.st1[j, 0:1, :], s.st1[j, 1:2, :]
+
+    def xh1(i):
+        return (s.xj[px(i), :].astype(f32) - mean1) * inv1
+
+    def make_dt1(i, carry):
+        n1 = xh1(i)
+        dt1 = da1_at(i) * slope_of(n1 * vec(0) + vec(1))
+        s.tmp[px(i), :] = dt1
+        return carry[0] + colsum(dt1), carry[1] + colsum(dt1 * n1)
+
+    dt1_sum, dt1_hat = each(make_dt1, (zero_row, zero_row))
+    m1c = group_sum(dt1_sum * vec(0)) * (1.0 / count)
+    m2c = group_sum(dt1_hat * vec(0)) * (1.0 / count)
+
+    def make_in(i):
+        v = s.dy1[px(i), :] + (s.tmp[px(i), :] * vec(0) - m1c - xh1(i) * m2c) * inv1
+        s.inj[px(i), :] = v.astype(bf16)
+
+    each(make_in)
+    in_copies = to_pixels(s.inj, in_grad)
+
+    qkv_sums = [each(lambda i, a, t=t: a + colsum(s.dqkv[t, px(i), :].astype(f32)), zero_row) for t in range(3)]
+    s.gvec[...] = jnp.concatenate(
+        [dt1_hat, dt1_sum, dh1_sum, scale * du_hat, scale * du_sum, dh2_sum, dn_hat, dn_sum, dy_sum]
+        + qkv_sums
+        + [colsum(s.dK[P : P + B, :]), colsum(s.dV[P : P + B, :]), dscale, du_sum],
+        axis=0,
+    )
+    gv_copies = [send(s.gvec, s.gvs.at[d], device) for device in dp_peers]
+    s.gvs[d] = s.gvec[...]
+    sum_z(c1)
+    for copy in gv_copies:
+        copy.wait_recv()
+    total = s.gvs[0]
+    for k in range(1, N):
+        total = total + s.gvs[k]
+    s.gvt[...] = total
+    s.gvi[j] = total
+    gv_copies = [send(s.gvt, s.gvi.at[j], device) for device in img_peers]
+    sum_img(c2)
+    sum_end(wq, g_q)
+    sum_end(wc, g_c)
+    sum_end(wo, g_o)
+    for copy in ds_copies:
+        copy.wait_recv()
+    e_cols = jnp.concatenate([s.eall[k, :, e_at] for k in range(N)], axis=0)
+    for t in range(2):
+        for k in range(J):
+            rows = jnp.concatenate([s.dsall[i, k, t : t + 1, :] for i in range(N)], axis=0)
+            v = lax.dot_general(
+                e_cols, rows, (((0,), (0,)), ((), ())), precision=highest, preferred_element_type=f32
+            )
+            s.geb[:, t * C + k * B : t * C + (k + 1) * B] = v
+    g_emb[...] = s.geb[rows_at(lax.rem(flat, 2) * RE, RE, 8), :]
+    for copy in gv_copies:
+        copy.wait_recv()
+    VW = g.VW
+    each_block = B // VW
+    pick = lax.broadcasted_iota(jnp.int32, (B, VW), 0) == (
+        lax.broadcasted_iota(jnp.int32, (B, VW), 1) + lax.rem(flat, each_block) * VW
+    )
+    g_v[...] = jnp.dot(
+        s.gvi[lax.div(flat, each_block)], jnp.where(pick, 1.0, 0.0), precision=highest,
+        preferred_element_type=f32,
+    )
+    sum_end(c2, gc2)
+    sum_img(c1)
+    sum_end(c1, gc1)
+    for copy in out_copies + in_copies:
+        copy.wait_recv()
+    wires.drain()
+
+
+def fused(
+    image, cond, context, w_conv1, w_conv2, w_embed, w_qkv, w_context, w_out, vectors, cotangent
+):
+    J, N = lax.axis_size("img"), lax.axis_size("dp")
+    local, cols, chans = image.shape[1:]
+    g = types.SimpleNamespace(
+        P=local * cols * J, Q=local * cols, C=chans, B=chans // J, N=N, J=J, COLS=cols, SIZE=chans // GROUPS,
+        T=context.shape[1], X=context.shape[2], E=cond.shape[1], RE=w_embed.shape[0], VW=vectors.shape[1],
+        HEAD=HEAD, FACTOR=HEAD ** (-0.5),
+        weights=[
+            (1, w_conv1.shape[0]), (1, w_conv2.shape[0]), (3, w_qkv.shape[0]), (2, w_context.shape[0]),
+            (1, w_out.shape[0]),
+        ],
+    )
+    groups = scratch_plan(g)
+    rows = local * cols
+    shape = jax.ShapeDtypeStruct
+    outs = [
+        shape((rows, chans), bf16), shape((rows, chans), bf16), shape(w_conv1.shape, f32), shape(w_conv2.shape, f32),
+        shape(w_embed.shape, f32), shape(w_qkv.shape, f32), shape(w_context.shape, f32), shape(w_out.shape, f32),
+        shape(vectors.shape, f32),
+    ]
+    copies = 256
+    vmem = pl.BlockSpec(memory_space=pltpu.VMEM)
+    result = pl.pallas_call(
+        functools.partial(body, g, groups),
+        out_shape=outs,
+        in_specs=[vmem] * 11,
+        out_specs=[vmem] * 9,
+        scratch_shapes=[pltpu.VMEM(*spec) for group in groups for spec in group.values()]
+        + [pltpu.SemaphoreType.DMA((copies,)), pltpu.SemaphoreType.DMA((copies,))],
+        compiler_params=pltpu.CompilerParams(
+            collective_id=0, has_side_effects=True, vmem_limit_bytes=60 * 1024 * 1024
+        ),
+    )(
+        image.reshape(rows, chans), cond, context[0], w_conv1, w_conv2, w_embed, w_qkv, w_context, w_out, vectors,
+        cotangent.reshape(rows, chans),
+    )
+    return (result[0].reshape(image.shape), result[1].reshape(image.shape), *result[2:])
 
 
 def on_device(
@@ -66,6 +844,13 @@
     width = chans // parts
     size = chans // GROUPS
     count = images * parts
+
+    if parts == 4 and width == 128 and images % 2 == 0 and all(
+        w.shape[0] % 16 == 0 for w in (w_conv1, w_conv2, w_embed, w_qkv, w_context, w_out)
+    ):
+        return fused(
+            image, cond, context, w_conv1, w_conv2, w_embed, w_qkv, w_context, w_out, vectors, cotangent
+        )
 
     def own(full):
         return lax.dynamic_slice_in_dim(full, place * width, width, full.ndim - 1)

time: 491 us -> 182 us (0.37); the launches traced: 483 us -> 181 us
  Pallas kernels: 0 us -> 171 us
  waiting for transfers between devices: 160 us -> 0 us
  local copies, waits for them, and re-layouts: 113 us -> 8.56 us
  blocking collectives: 94.4 us -> 0 us
  matrix products: 47.8 us -> 0 us
  other arithmetic: 38.9 us -> 0 us
  between operations: 16 us -> 0.67 us
  starting transfers between devices: 11.9 us -> 0 us
    pallas_call x0 -> x1, Pallas kernels: none -> 171 us  [fused(): pl.pallas_call(functools.partial(body, g, groups), out_shape=outs, in_spe...]
    reduce_scatter x1 -> x0, waiting for transfers between devices: 78.9 us -> none  [on_device(): lax.psum_scatter(packed, 'dp', scatter_dimension=0, tiled=True).astype(f32)]
    all_gather x3 -> x0, blocking collectives: 54.3 us -> none  [the longest x1 41.9 us: on_device(): lax.all_gather(vectors, ('dp', 'img'), axis=1, tiled=True).astype(f32)]
    dot_general x27 -> x0, matrix products: 47.8 us -> none  [the longest x20 30.6 us: dot(): return jnp.dot(a, b, preferred_element_type=f32)]
    all_gather x5 -> x0, waiting for transfers between devices: 38.1 us -> none  [the longest x1 24.9 us: on_device(): packed = lax.all_gather(packed, 'dp', axis=0, tiled=True)]
    unnamed x12 -> x0, waiting for transfers between devices: 30.1 us -> none
    unnamed x227 -> x25, local copies, waits for them, and re-layouts: 36.1 us -> 8.56 us
    reduce_sum x29 -> x0, other arithmetic: 23.4 us -> none  [the longest x2 3.47 us: on_device(): jnp.sum(v, 0)]
  transfers between devices with their start and end apart: 12 -> 0, of which waited for: 7 -> 0; matrix products, arithmetic and copies ran while one was open for 27% -> 0% of each run, Pallas kernels for 0% -> 0%
where the time goes in v2:
time: 182 us; the launch traced here: 181 us
  Pallas kernels  171 us (94%)
  local copies, waits for them, and re-layouts  8.56 us (5%)
    pallas_call x1, Pallas kernels, fused(): pl.pallas_call(functools.partial(body, g, groups), out_shape=outs, in_spe...  171 us
    unnamed x25, local copies, waits for them, and re-layouts  8.56 us

profile of v2, /device:TPU:0, one launch (start us, length us, event | category | flops | bytes accessed | tf_op | source)
XLA Modules:
  0.0 180.7 jit_solution(11632972652085202438)
XLA Ops:
  0.6 171.5 %shard_map.178 = (bf16[256,512]{1,0:T(8,128)(2,1)}, bf16[256,512]{1,0:T(8,128)(2,1)}, f32[144,512]{1,0:T(8,128)}, f32[144,512]{1,0:T(8,128)}, f32[64,1024]{1,0:T...) custom-call(bf16[256,512]{1,0:T(8,128)(2,1)} %bitcast.8, ...), custom_call_target="tpu_custom_call" | custom-call | tf_op jit(solution)/shard_map/pallas_call | solution.py:819
  172.1 0.0 copy-start.4
  172.1 1.7 copy.29
  173.8 0.0 copy-done.4
  173.8 0.0 copy-start.1
  173.9 0.7 copy.30
  174.6 0.4 copy-done.1
  174.9 0.0 copy-start
  174.9 0.7 copy.31
  175.6 0.4 copy-done
  176.0 0.7 copy.32
  176.7 0.3 copy-done.3
  177.0 0.0 copy-start.5
  177.0 0.7 copy.33
  177.7 0.3 copy-done.5
  178.0 0.6 copy.34
  178.6 0.0 copy-done.2
  178.6 0.0 copy-start.6
  178.6 0.7 copy.35
  179.3 0.1 copy-done.6
  179.4 0.0 copy-start.7
  179.4 0.6 copy.36
  180.0 0.1 copy-done.7
  180.1 0.6 copy.37
  (2 shorter events, 0.0 us)
Async XLA Ops:
  172.1 1.7 copy-start.4
  173.8 1.1 copy-start.1
  174.9 1.1 copy-start
  176.0 1.1 copy-start.3
  177.0 1.0 copy-start.5
  177.0 1.6 copy-start.2
  178.6 0.8 copy-start.6
  179.4 0.7 copy-start.7

commit v3 on v2

--- a/solution.py
+++ b/solution.py
@@ -62,21 +62,36 @@
 
 class Wires:
     def __init__(self, sent, landed):
-        self.sent, self.landed, self.copies = sent, landed, []
-
-    def send(self, source, target, device):
-        at = len(self.copies)
-        copy = pltpu.make_async_remote_copy(
-            src_ref=source, dst_ref=target, send_sem=self.sent.at[at], recv_sem=self.landed.at[at],
+        self.sent, self.landed, self.used, self.held = sent, landed, [0, 0], []
+
+    def slot(self, kind, count=1):
+        self.used[kind] += count
+        return self.used[kind] - count
+
+    def copy(self, out, at, source, target, device):
+        return pltpu.make_async_remote_copy(
+            src_ref=source, dst_ref=target, send_sem=self.sent.at[out], recv_sem=self.landed.at[at],
             device_id=device, device_id_type=pl.DeviceIdType.MESH,
         )
+
+    def send(self, source, target, device, out=None):
+        copy = self.copy(self.slot(0) if out is None else out, self.slot(1), source, target, device)
         copy.start()
-        self.copies.append(copy)
+        if out is None:
+            self.held.append(copy.wait_send)
         return copy
 
+    def group(self, triples, whole):
+        out, at = self.slot(0), self.slot(1)
+        for source, target, device in triples:
+            self.copy(out, at, source, target, device).start()
+        total = self.copy(out, at, whole, whole, triples[0][2])
+        self.held.append(total.wait_send)
+        return total
+
     def drain(self):
-        for copy in self.copies:
-            copy.wait_send()
+        for finish in self.held:
+            finish()
 
 
 def scratch_plan(g):
@@ -92,7 +107,7 @@
         st1=((J, 8, B), f32), xj=((P, B), bf16),
         h1=((P, B), f32), y1=((P, B), f32), dy1=((P, B), f32), tmp=((P, B), f32),
         W1T=((2, 9 * B, 2 * B), bf16), W2T=((2, 9 * B, 2 * B), bf16), WqT=((2, 3 * B, 2 * B), bf16),
-        ctx=((B, X), bf16), ctxT=((X, B), bf16),
+        ctx=((B, X), bf16), ctxs=((N, B, X // N), bf16), dcx=((B, 2 * B), bf16), dcxs=((N, B, 2 * B), bf16),
         Kb=((P + B, B), bf16), Vb=((P + B, B), bf16), KT=((B, P + B), bf16), VT=((B, P + B), bf16),
         qs=((P, B), bf16), dK=((P + B, B), f32), dV=((P + B, B), f32), dqkv=((3, P, B), bf16),
         WoF=((2, C, 2 * B), bf16), dopx=((Q, C), bf16), doj=((P, B), bf16), dyj=((P, B), bf16),
@@ -105,10 +120,12 @@
     groups = [plan, half, half, half]
     for wide, rows in g.weights:
         depth = rows * J
+        summed = {} if wide == 2 else dict(
+            g=((wide, depth * N, B), bf16), rx=((N // 2, wide, depth, B), bf16), zs=((N // 2, wide, depth, B), bf16),
+            zr=((N // 2, wide, depth, B), bf16),
+        )
         groups.append(dict(
-            w=((wide, depth * N, B), bf16), g=((wide, depth * N, B), bf16),
-            rx=((N // 2, wide, depth, B), bf16), zs=((N // 2, wide, depth, B), bf16),
-            zr=((N // 2, wide, depth, B), bf16), fin=((wide, depth, B), bf16), gr=((J, wide, rows, B), bf16),
+            w=((wide, depth * N, B), bf16), fin=((wide, depth, B), bf16), gr=((J, wide, rows, B), bf16), **summed
         ))
     return groups
 
@@ -126,10 +143,11 @@
     rest = (wq, wc, wo)
     P, Q, C, B, N, J, COLS, SIZE = g.P, g.Q, g.C, g.B, g.N, g.J, g.COLS, g.SIZE
     T, E, RE = g.T, g.E, g.RE
+    XN, TP = g.X // N, (T + 15) // 16 * 16
     Z = N // 2
     STEPS = P // Q
     wires = Wires(refs[-2], refs[-1])
-    send = wires.send
+    send, group = wires.send, wires.group
     d = lax.axis_index("dp")
     j = lax.axis_index("img")
     flat = d * J + j
@@ -177,6 +195,9 @@
         return v[0:1]
 
     def colsum(v):
+        while v.shape[0] % 32 == 0:
+            half = v.shape[0] // 2
+            v = v[:half] + v[half:]
         return jnp.sum(v, axis=0, keepdims=True)
 
     zero_row = jnp.zeros((1, B), f32)
@@ -214,11 +235,14 @@
 
     def stage_img(W):
         start = d * W.depth + j * W.rows
-        W.img = []
-        for device in img_peers:
-            for t in range(W.wide):
-                source = W.ref.at[:, rows_at(t * C + device[1] * B, B, B)]
-                W.img.append(send(source, W.w.at[t, rows_at(start, W.rows, 16), :], device))
+        W.img = group(
+            [
+                (W.ref.at[:, rows_at(t * C + device[1] * B, B, B)], W.w.at[t, rows_at(start, W.rows, 16), :], device)
+                for device in img_peers
+                for t in range(W.wide)
+            ],
+            W.w.at[:, 0 : (J - 1) * W.rows, :],
+        )
 
     def own_img(W):
         start = d * W.depth + j * W.rows
@@ -228,22 +252,65 @@
     def block(W, ref, owner):
         return ref.at[:, rows_at(owner * W.depth, W.depth, 16), :]
 
-    def stage_z(W):
-        for copy in W.img:
-            copy.wait_recv()
-        mine = block(W, W.w, d)
-        W.z = [send(mine, mine, (zdev[k] * 2 + xx, j)) for k in range(1, Z)]
-        W.x = [send(mine, mine, xpeer)]
-
-    def forward(W):
-        for k, copy in enumerate(W.z, 1):
-            copy.wait_recv()
-            here = block(W, W.w, zsrc[k] * 2 + xx)
-            W.x.append(send(here, here, xpeer))
-
-    def arrive(W):
-        for copy in W.x:
-            copy.wait_recv()
+    def img_done(W):
+        W.img.wait_recv()
+
+    above, below = z < Z - 1, z > 0
+    up, down = ((z + 1) * 2 + xx, j), ((z - 1) * 2 + xx, j)
+
+    def piece(W, start, size):
+        p = types.SimpleNamespace(W=W, start=start, size=size)
+        p.zr, p.xr, p.zs, p.xs = wires.slot(1, Z), wires.slot(1), wires.slot(0), wires.slot(0)
+        p.at = lambda owner: W.w.at[:, rows_at(owner * W.depth + start, size, 16), :]
+        p.first = lambda count: W.w.at[:, 0 : count * size, :]
+
+        def finish():
+            wires.copy(p.xs, p.xr, p.first(Z), p.first(Z), xpeer).wait_send()
+            for count, gate in ((Z + 1, above & below), (1, (z == 0) | (z == Z - 1))):
+                pl.when(gate)(
+                    lambda: wires.copy(p.zs, p.xr, p.first(count), p.first(count), xpeer).wait_send()
+                )
+
+        wires.held.append(finish)
+        return p
+
+    def move(p, owner, device):
+        here = p.at(owner * 2 + xx)
+        wires.copy(p.zs, p.zr + owner, here, here, device).start()
+
+    def across(p, owner):
+        here = p.at(owner * 2 + xx)
+        wires.copy(p.xs, p.xr, here, here, xpeer).start()
+
+    def z_start(pieces):
+        for p in pieces:
+            pl.when(above)(lambda: move(p, z, up))
+            pl.when(below)(lambda: move(p, z, down))
+        for p in pieces:
+            across(p, z)
+
+    def z_step(pieces, step):
+        def take(owner, onward, device):
+            for p in pieces:
+                here = p.at(owner * 2 + xx)
+                wires.copy(p.zs, p.zr + owner, here, here, xpeer).wait_recv()
+                if step < Z - 1:
+                    pl.when(onward)(lambda: move(p, owner, device))
+                across(p, owner)
+
+        pl.when(z >= step)(lambda: take(z - step, above, up))
+        pl.when(z + step < Z)(lambda: take(z + step, below, down))
+
+    def arrive(pieces):
+        for p in pieces:
+            wires.copy(p.xs, p.xr, p.first(Z), p.first(Z), xpeer).wait_recv()
+
+    def halves(W):
+        half = W.depth // 32 * 16
+        return [piece(W, 0, half), piece(W, half, W.depth - half)]
+
+    p1, p2 = halves(c1), halves(c2)
+    pq, pc, po = ([piece(W, 0, W.depth)] for W in rest)
 
     def gather_start(mine):
         return types.SimpleNamespace(y=send(mine, mine, ypeer), c=send(mine, mine, sib))
@@ -259,10 +326,11 @@
         state.f.wait_recv()
 
     stage_img(c1)
-    v_stage1 = [send(s.vown, s.vs1.at[j], device) for device in img_peers]
+    stage_img(wo)
+    v_stage1 = group([(s.vown, s.vs1.at[j], device) for device in img_peers], s.vs1.at[0 : J - 1])
     x_own = s.X.at[j]
     x_state = types.SimpleNamespace(y=send(x_in, x_own, ypeer), c=send(x_in, x_own, sib))
-    e_stage1 = [send(s.eall.at[d], s.eall.at[d], device) for device in dp_peers]
+    e_stage1 = group([(s.eall.at[d], s.eall.at[d], device) for device in dp_peers], s.eall.at[0 : N - 1])
     own_img(c1)
     s.X[j] = x_in[...]
     for W in (c2, *rest):
@@ -276,28 +344,37 @@
         s.S[c, P + COLS : P + 2 * COLS, :] = jnp.zeros((COLS, B), bf16)
     s.ctx[...] = jnp.zeros((B, g.X), bf16)
     s.ctx[0:T, :] = ctx_in[...]
-    stage_z(c1)
-    for copy in v_stage1:
-        copy.wait_recv()
+    if TP < B:
+        s.ctxs[:, TP:B, :] = jnp.zeros((N, B - TP, XN), bf16)
+        s.dcxs[:, TP:B, :] = jnp.zeros((N, B - TP, 2 * B), bf16)
+    img_done(c1)
+    z_start(p1[:1])
+    z_start(p1[1:])
+    img_done(wo)
+    z_start(po)
+    v_stage1.wait_recv()
     total = s.vs1[0].astype(f32)
     for k in range(1, J):
         total = total + s.vs1[k].astype(f32)
     s.vsum[...] = total.astype(bf16)
     s.vs2[d] = total.astype(bf16)
-    v_stage2 = [send(s.vsum, s.vs2.at[d], device) for device in dp_peers]
+    v_stage2 = group([(s.vsum, s.vs2.at[d], device) for device in dp_peers], s.vs2.at[0 : N - 1])
+    stage_img(c2)
 
     x_state.y.wait_recv()
     far = s.X.at[(1 - yy) * 2 + cc]
     x_state.f = send(far, far, sib)
-    for W in (c2, *rest):
-        stage_img(W)
-    dy_copies = [
-        send(dy_in.at[:, lanes(device[1])], s.dyj.at[rows_at(j * Q, Q, Q), :], device) for device in img_peers
-    ]
+    stage_img(wq)
+    stage_img(wc)
+    dy_copies = group(
+        [(dy_in.at[:, lanes(device[1])], s.dyj.at[rows_at(j * Q, Q, Q), :], device) for device in img_peers],
+        s.dyj.at[0 : P - Q, :],
+    )
     s.dyj[rows_at(j * Q, Q, Q), :] = dy_in[:, lanes(j)]
-
-    for copy in e_stage1:
-        copy.wait_recv()
+    z_step(p1[:1], 1)
+    z_step(p1[1:] + po, 1)
+
+    e_stage1.wait_recv()
     s.wemb[...] = jnp.zeros((2 * RE, 2 * C), bf16)
     s.wemb[rows_at(lax.rem(flat, 2) * RE, RE, 16), :] = w_emb[...]
     e_at = rows_at(lax.div(flat, 2) * (2 * RE), 2 * RE, B)
@@ -306,7 +383,7 @@
     for k in range(N):
         s.epart[k] = part[k : k + 1]
     s.erx[d] = s.epart[d]
-    e_stage2 = [send(s.epart.at[device[0]], s.erx.at[d], device) for device in dp_peers]
+    e_stage2 = group([(s.epart.at[device[0]], s.erx.at[d], device) for device in dp_peers], s.erx.at[0 : N - 1])
 
     x_state.c.wait_recv()
     x_state.f.wait_recv()
@@ -314,19 +391,27 @@
     def load_x(k):
         return lambda i: s.X[i, :, k * B : (k + 1) * B].astype(f32)
 
-    for k in range(J):
+    def stats(k):
         mean, inverse = moments(load_x(k))
         s.st1[k, 0:1, :] = mean
         s.st1[k, 1:2, :] = inverse
-    for copy in e_stage2:
-        copy.wait_recv()
+
+    stats(0)
+    stats(1)
+    z_step(p1[:1], 2)
+    z_step(p1[1:] + po, 2)
+    img_done(c2)
+    z_start(p2[:1])
+    z_start(p2[1:])
+    stats(2)
+    stats(3)
+    e_stage2.wait_recv()
     total = s.erx[0]
     for k in range(1, N):
         total = total + s.erx[k]
     s.esum[j] = total
-    e_stage3 = [send(s.esum.at[j], s.esum.at[j], device) for device in img_peers]
-    for copy in v_stage2:
-        copy.wait_recv()
+    e_stage3 = group([(s.esum.at[j], s.esum.at[j], device) for device in img_peers], s.esum.at[0 : J - 1])
+    v_stage2.wait_recv()
     total = s.vs2[0].astype(f32)
     for k in range(1, N):
         total = total + s.vs2[k].astype(f32)
@@ -336,7 +421,8 @@
     def vec(row):
         return s.vecs[j, row : row + 1, :]
 
-    forward(c1)
+    z_step(p1[:1], 3)
+    z_step(p1[1:] + po, 3)
     for k in range(J):
         mean, inverse = s.st1[k, 0:1, :], s.st1[k, 1:2, :]
         gain, bias = s.vecs[k, 0:1, :], s.vecs[k, 1:2, :]
@@ -357,17 +443,20 @@
         each(one)
 
     each(lambda i: s.xj.__setitem__((px(i), slice(None)), s.X[i, :, lanes(j)]))
-    turn(s.A1, s.A1T, COLS)
-    for copy in e_stage3:
-        copy.wait_recv()
+    z_step(p2[:1], 1)
+    z_step(p2[1:], 1)
+    e_stage3.wait_recv()
     total = s.esum[0]
     for k in range(1, J):
         total = total + s.esum[k]
     s.emb[...] = total
     scale = 1.0 + (s.emb[:, lanes(j)] + vec(14))
     shift = s.emb[:, lanes(j + J)] + vec(15)
-    stage_z(c2)
-    arrive(c1)
+    arrive(po)
+    wo_at = s.WoF.at[yy, :, lanes(cc)]
+    s.WoF[yy, :, lanes(cc)] = wo.w[0]
+    wo_state = gather_start(wo_at)
+    arrive(p1)
 
     def convolve(A, W, emit):
         def one(i):
@@ -390,6 +479,9 @@
 
     convolve(s.A1, c1.w, save_h1)
     mean2, inv2 = moments(lambda i: s.h1[px(i), :])
+    gather_far(wo_state, s.WoF.at[1 - yy, :, lanes(cc)])
+    gather_near(wo_state)
+    gather_end(wo_state)
 
     def xh2(i):
         return (s.h1[px(i), :] - mean2) * inv2
@@ -404,13 +496,30 @@
     each(act2)
     inside = pl.ds(COLS, P)
     a2_state = gather_start(s.A2.at[yy, inside, lanes(cc)])
-    forward(c2)
-    for W in rest:
-        stage_z(W)
+    for h in range(2):
+        part = mm_t(dy_in[:, 0 : 2 * B], s.WoF[0, h * 2 * B : (h + 1) * 2 * B, :])
+        part = part + mm_t(dy_in[:, 2 * B : 4 * B], s.WoF[1, h * 2 * B : (h + 1) * 2 * B, :])
+        s.dopx[:, h * 2 * B : (h + 1) * 2 * B] = part.astype(bf16)
+    do_copies = group(
+        [(s.dopx.at[:, lanes(device[1])], s.doj.at[rows_at(j * Q, Q, Q), :], device) for device in img_peers],
+        s.doj.at[0 : P - Q, :],
+    )
+    s.doj[rows_at(j * Q, Q, Q), :] = s.dopx[:, lanes(j)]
+    z_step(p2[:1], 2)
+    z_step(p2[1:], 2)
+    img_done(wq)
+    img_done(wc)
+    z_start(pq)
+    z_start(pc)
+    z_step(p2[:1], 3)
+    z_step(p2[1:], 3)
     gather_far(a2_state, s.A2.at[1 - yy, inside, lanes(cc)])
+    turn(s.A1, s.A1T, COLS)
+    z_step(pq, 1)
+    z_step(pc, 1)
     gather_near(a2_state)
     gather_end(a2_state)
-    arrive(c2)
+    arrive(p2)
 
     def save_y1(i, v):
         s.y1[px(i), :] = s.xj[px(i), :].astype(f32) + v + vec(5)
@@ -426,8 +535,8 @@
 
     each(act3)
     n_state = gather_start(s.N3.at[yy, :, lanes(cc)])
-    for W in rest:
-        forward(W)
+    z_step(pq, 2)
+    z_step(pc, 2)
     turn(s.A2, s.A2T, COLS)
 
     def turn_weights(W, target, taps, stride):
@@ -441,32 +550,27 @@
 
     turn_weights(conv_tap(c2), s.W2T, 9, C)
     gather_far(n_state, s.N3.at[1 - yy, :, lanes(cc)])
+    z_step(pq, 3)
+    z_step(pc, 3)
     turn_weights(conv_tap(c1), s.W1T, 9, C)
-    s.ctxT[...] = s.ctx[...].T
-    for W in rest:
-        arrive(W)
-    wo_at = s.WoF.at[yy, :, lanes(cc)]
-    s.WoF[yy, :, lanes(cc)] = wo.w[0]
-    wo_state = gather_start(wo_at)
+    arrive(pq)
+    arrive(pc)
     turn_weights(lambda t: wq.w.at[t], s.WqT, 3, C)
     tokens = lax.broadcasted_iota(jnp.int32, (B, B), 0) < T
     for t, target in enumerate((s.Kb, s.Vb)):
         v = mm(s.ctx[...], wc.w[t]) + vec(12 + t)
         target[P : P + B, :] = jnp.where(tokens, v, 0.0).astype(bf16)
-    gather_far(wo_state, s.WoF.at[1 - yy, :, lanes(cc)])
-    gather_near(wo_state)
-    gather_end(wo_state)
-    for h in range(2):
-        part = mm_t(dy_in[:, 0 : 2 * B], s.WoF[0, h * 2 * B : (h + 1) * 2 * B, :])
-        part = part + mm_t(dy_in[:, 2 * B : 4 * B], s.WoF[1, h * 2 * B : (h + 1) * 2 * B, :])
-        s.dopx[:, h * 2 * B : (h + 1) * 2 * B] = part.astype(bf16)
-    do_copies = [
-        send(s.dopx.at[:, lanes(device[1])], s.doj.at[rows_at(j * Q, Q, Q), :], device)
-        for device in img_peers
-    ]
-    s.doj[rows_at(j * Q, Q, Q), :] = s.dopx[:, lanes(j)]
     gather_near(n_state)
     gather_end(n_state)
+
+    def tokens_of(owner):
+        return s.ctx.at[0:TP, rows_at(owner * XN, XN, B)]
+
+    ctx_copies = group(
+        [(tokens_of(device[0]), s.ctxs.at[d, 0:TP, :], device) for device in dp_peers],
+        s.ctxs.at[0 : N - 1, 0:TP, :],
+    )
+    s.ctxs[d, 0:TP, :] = tokens_of(d)[...]
 
     def project(i):
         left = jnp.concatenate([s.N3[0, px(i), :], s.N3[1, px(i), :]], axis=1)
@@ -481,8 +585,8 @@
     for source, target in ((s.Kb, s.KT), (s.Vb, s.VT)):
         for k in range(0, P + B, B):
             target[:, k : k + B] = source[k : k + B, :].T
-    for copy in do_copies + dy_copies:
-        copy.wait_recv()
+    do_copies.wait_recv()
+    dy_copies.wait_recv()
     s.dK[...] = jnp.zeros((P + B, B), f32)
     s.dV[...] = jnp.zeros((P + B, B), f32)
 
@@ -561,35 +665,47 @@
     order = list(range(1, Z)) + [0]
 
     def sum_start(W):
-        W.sx = {}
+        W.sx, W.zout, W.zin = {}, wires.slot(0), wires.slot(1)
+        out = wires.slot(0)
         for k in order:
-            W.sx[k] = send(block(W, W.g, zdev[k] * 2 + (1 - xx)), W.rx.at[k], xpeer)
+            W.sx[k] = send(block(W, W.g, zdev[k] * 2 + (1 - xx)), W.rx.at[k], xpeer, out)
+        wires.held.append(wires.copy(out, W.zin, W.rx, W.rx, xpeer).wait_send)
+
+    def sum_block(W, k):
+        W.sx[k].wait_recv()
+        at = rows_at((zdev[k] * 2 + xx) * W.depth, W.depth, 16)
+        v = W.g[:, at, :].astype(f32) + W.rx[k].astype(f32)
+        W.zs[k] = v.astype(bf16)
+        if k:
+            wires.copy(W.zout, W.zin, W.zs.at[k], W.zr.at[k], (zdev[k] * 2 + xx, j)).start()
 
     def sum_z(W):
-        W.sz = {}
         for k in order:
-            W.sx[k].wait_recv()
-            at = rows_at((zdev[k] * 2 + xx) * W.depth, W.depth, 16)
-            v = W.g[:, at, :].astype(f32) + W.rx[k].astype(f32)
-            W.zs[k] = v.astype(bf16)
-            if k:
-                W.sz[k] = send(W.zs.at[k], W.zr.at[k], (zdev[k] * 2 + xx, j))
+            sum_block(W, k)
 
     def sum_img(W):
+        total = wires.copy(W.zout, W.zin, W.zr.at[0 : Z - 1], W.zr.at[0 : Z - 1], xpeer)
+        total.wait_recv()
+        wires.held.append(total.wait_send)
         v = W.zs[0].astype(f32)
         for k in range(1, Z):
-            W.sz[k].wait_recv()
             v = v + W.zr[k].astype(f32)
-        W.fin[...] = v.astype(bf16)
-        W.simg = [
-            send(W.fin.at[:, rows_at(device[1] * W.rows, W.rows, 16), :], W.gr.at[j], device)
-            for device in img_peers
-        ]
+        to_rows(W, jnp.concatenate([v[t] for t in range(W.wide)], axis=1))
+
+    def to_rows(W, v):
+        for t in range(W.wide):
+            W.fin[t] = v[:, t * B : (t + 1) * B].astype(bf16)
+        W.simg = group(
+            [
+                (W.fin.at[:, rows_at(device[1] * W.rows, W.rows, 16), :], W.gr.at[j], device)
+                for device in img_peers
+            ],
+            W.gr.at[0 : J - 1],
+        )
         W.gr[j] = W.fin[:, rows_at(j * W.rows, W.rows, 16), :]
 
     def sum_end(W, target):
-        for copy in W.simg:
-            copy.wait_recv()
+        W.simg.wait_recv()
         for k in range(J):
             for t in range(W.wide):
                 target[:, t * C + k * B : t * C + (k + 1) * B] = W.gr[k, t].astype(f32)
@@ -604,13 +720,12 @@
         for t in range(3):
             wq.g[t, at, :] = v[:, t * B : (t + 1) * B]
     sum_start(wq)
-    d_ctx = jnp.concatenate([s.dK[P : P + B, :], s.dV[P : P + B, :]], axis=1).astype(bf16)
-    X_ = g.X
-    for k in range(0, X_, C):
-        v = mm(s.ctxT[k : k + C, :], d_ctx).astype(bf16)
-        wc.g[0, k : k + C, :] = v[:, :B]
-        wc.g[1, k : k + C, :] = v[:, B:]
-    sum_start(wc)
+    s.dcx[...] = jnp.concatenate([s.dK[P : P + B, :], s.dV[P : P + B, :]], axis=1).astype(bf16)
+    s.dcxs[d] = s.dcx[...]
+    dcx_copies = group(
+        [(s.dcx.at[0:TP, :], s.dcxs.at[d, 0:TP, :], device) for device in dp_peers],
+        s.dcxs.at[0 : N - 1, 0:TP, :],
+    )
     gather_far(o_state, s.O.at[1 - yy, :, lanes(cc)])
     gather_near(o_state)
     gather_end(o_state)
@@ -622,9 +737,10 @@
     each(finish)
 
     def to_pixels(source, target):
-        copies = [
-            send(source.at[rows_at(device[1] * Q, Q, Q), :], target.at[:, lanes(j)], device) for device in img_peers
-        ]
+        copies = group(
+            [(source.at[rows_at(device[1] * Q, Q, Q), :], target.at[:, lanes(j)], device) for device in img_peers],
+            source.at[0 : P - Q, :],
+        )
         target[:, lanes(j)] = source[rows_at(j * Q, Q, Q), :]
         return copies
 
@@ -643,6 +759,7 @@
         return first, second, group_sum(first * factor) * (1.0 / count), group_sum(second * factor) * (1.0 / count)
 
     dn_done()
+    sum_z(wq)
     dn_sum, dn_hat, m1, m2 = back_sums(dn_at, xh3, vec(6))
 
     def shifted(i, v):
@@ -677,10 +794,15 @@
 
     da2_done, da2_at = scatter(da2_bufs, field, s.W2T)
     kernel_grad(c2, s.A2T)
-    sum_z(wq)
-    sum_z(wc)
+    sum_start(c2)
     sum_z(wo)
-    sum_start(c2)
+    ctx_copies.wait_recv()
+    dcx_copies.wait_recv()
+    v = lax.dot_general(
+        s.ctxs[...].reshape(N * B, XN), s.dcxs[...].reshape(N * B, 2 * B), (((0,), (0,)), ((), ())),
+        preferred_element_type=f32,
+    )
+    to_rows(wc, v)
     da2_done()
 
     def slope_of(v):
@@ -705,18 +827,17 @@
 
     dh1_sum = each(make_dh1, zero_row)
     dscale = vec(3) * du_hat + vec(4) * du_sum
-    da1_done, da1_at = scatter(da1_bufs, field, s.W1T)
     kernel_grad(c1, s.A1T)
     sum_start(c1)
+    da1_done, da1_at = scatter(da1_bufs, field, s.W1T)
     s.dse[j] = jnp.concatenate([dscale, du_sum], axis=0)
-    ds_copies = [send(s.dse.at[j], s.dse.at[j], device) for device in img_peers]
-    for W in rest:
-        sum_img(W)
+    ds_copies = group([(s.dse.at[j], s.dse.at[j], device) for device in img_peers], s.dse.at[0 : J - 1])
+    sum_img(wq)
+    sum_img(wo)
     sum_z(c2)
-    for copy in ds_copies:
-        copy.wait_recv()
+    ds_copies.wait_recv()
     s.dsall[d] = s.dse[...]
-    ds_copies = [send(s.dse, s.dsall.at[d], device) for device in dp_peers]
+    ds_copies = group([(s.dse, s.dsall.at[d], device) for device in dp_peers], s.dsall.at[0 : N - 1])
     da1_done()
     mean1, inv1 = s.st1[j, 0:1, :], s.st1[j, 1:2, :]
 
@@ -747,23 +868,21 @@
         + [colsum(s.dK[P : P + B, :]), colsum(s.dV[P : P + B, :]), dscale, du_sum],
         axis=0,
     )
-    gv_copies = [send(s.gvec, s.gvs.at[d], device) for device in dp_peers]
+    gv_copies = group([(s.gvec, s.gvs.at[d], device) for device in dp_peers], s.gvs.at[0 : N - 1])
     s.gvs[d] = s.gvec[...]
     sum_z(c1)
-    for copy in gv_copies:
-        copy.wait_recv()
+    gv_copies.wait_recv()
     total = s.gvs[0]
     for k in range(1, N):
         total = total + s.gvs[k]
     s.gvt[...] = total
     s.gvi[j] = total
-    gv_copies = [send(s.gvt, s.gvi.at[j], device) for device in img_peers]
+    gv_copies = group([(s.gvt, s.gvi.at[j], device) for device in img_peers], s.gvi.at[0 : J - 1])
     sum_img(c2)
     sum_end(wq, g_q)
     sum_end(wc, g_c)
     sum_end(wo, g_o)
-    for copy in ds_copies:
-        copy.wait_recv()
+    ds_copies.wait_recv()
     e_cols = jnp.concatenate([s.eall[k, :, e_at] for k in range(N)], axis=0)
     for t in range(2):
         for k in range(J):
@@ -773,8 +892,7 @@
             )
             s.geb[:, t * C + k * B : t * C + (k + 1) * B] = v
     g_emb[...] = s.geb[rows_at(lax.rem(flat, 2) * RE, RE, 8), :]
-    for copy in gv_copies:
-        copy.wait_recv()
+    gv_copies.wait_recv()
     VW = g.VW
     each_block = B // VW
     pick = lax.broadcasted_iota(jnp.int32, (B, VW), 0) == (
@@ -787,9 +905,10 @@
     sum_end(c2, gc2)
     sum_img(c1)
     sum_end(c1, gc1)
-    for copy in out_copies + in_copies:
-        copy.wait_recv()
+    out_copies.wait_recv()
+    in_copies.wait_recv()
     wires.drain()
+    assert wires.used[0] <= g.copies[0] and wires.used[1] <= g.copies[1], wires.used
 
 
 def fused(
@@ -814,7 +933,7 @@
         shape(w_embed.shape, f32), shape(w_qkv.shape, f32), shape(w_context.shape, f32), shape(w_out.shape, f32),
         shape(vectors.shape, f32),
     ]
-    copies = 256
+    g.copies = (71, 49 + 11 * (N // 2 + 1))
     vmem = pl.BlockSpec(memory_space=pltpu.VMEM)
     result = pl.pallas_call(
         functools.partial(body, g, groups),
@@ -822,7 +941,7 @@
         in_specs=[vmem] * 11,
         out_specs=[vmem] * 9,
         scratch_shapes=[pltpu.VMEM(*spec) for group in groups for spec in group.values()]
-        + [pltpu.SemaphoreType.DMA((copies,)), pltpu.SemaphoreType.DMA((copies,))],
+        + [pltpu.SemaphoreType.DMA((count,)) for count in g.copies],
         compiler_params=pltpu.CompilerParams(
             collective_id=0, has_side_effects=True, vmem_limit_bytes=60 * 1024 * 1024
         ),

time: 182 us -> 155 us (0.85)
  Pallas kernels: 171 us -> 145 us
    pallas_call x1, Pallas kernels: 171 us -> 145 us  [fused(): pl.pallas_call(functools.partial(body, g, groups), out_shape=outs, in_spe...]
where the time goes in v3:
time: 155 us; the launch traced here: 154 us
  Pallas kernels  145 us (94%)
  local copies, waits for them, and re-layouts  8.56 us (6%)
    pallas_call x1, Pallas kernels, fused(): pl.pallas_call(functools.partial(body, g, groups), out_shape=outs, in_spe...  145 us
    unnamed x25, local copies, waits for them, and re-layouts  8.56 us

profile of v3, /device:TPU:0, one launch (start us, length us, event | category | flops | bytes accessed | tf_op | source)
XLA Modules:
  0.0 154.4 jit_solution(11411365314807691392)
XLA Ops:
  0.6 145.2 %shard_map.178 = (bf16[256,512]{1,0:T(8,128)(2,1)}, bf16[256,512]{1,0:T(8,128)(2,1)}, f32[144,512]{1,0:T(8,128)}, f32[144,512]{1,0:T(8,128)}, f32[64,1024]{1,0:T...) custom-call(bf16[256,512]{1,0:T(8,128)(2,1)} %bitcast.8, ...), custom_call_target="tpu_custom_call" | custom-call | tf_op jit(solution)/shard_map/pallas_call | solution.py:938
  145.8 0.0 copy-start.4
  145.8 1.7 %copy.29 = bf16[1,4,64,512]{3,2,1,0:T(8,128)(2,1)} copy(bf16[1,4,64,512]{3,2,1,0:T(8,128)(2,1)} %bitcast.7) | data formatting | bytes 524288
  147.5 0.0 copy-done.4
  147.5 0.0 copy-start.1
  147.6 0.7 copy.30
  148.3 0.4 copy-done.1
  148.6 0.0 copy-start
  148.6 0.7 copy.31
  149.3 0.4 copy-done
  149.7 0.0 copy-start.3
  149.7 0.7 copy.32
  150.4 0.3 copy-done.3
  150.7 0.0 copy-start.5
  150.7 0.0 copy-start.2
  150.7 0.7 copy.33
  151.4 0.3 copy-done.5
  151.7 0.6 copy.34
  152.3 0.0 copy-done.2
  152.3 0.7 copy.35
  153.0 0.1 copy-done.6
  153.1 0.6 copy.36
  153.7 0.1 copy-done.7
  153.8 0.6 copy.37
  (2 shorter events, 0.0 us)
Async XLA Ops:
  145.8 1.7 %copy-start.4 = (bf16[256,512]{1,0:T(8,128)(2,1)S(1)}, bf16[256,512]{1,0:T(8,128)(2,1)}, u32[]{:S(2)}) copy-start(bf16[256,512]{1,0:T(8,128)(2,1)} %get-tuple-element.19) | copy-start | bytes 786436
  147.5 1.1 copy-start.1
  148.6 1.1 copy-start
  149.7 1.1 copy-start.3
  150.7 1.0 copy-start.5
  150.7 1.6 %copy-start.2 = (f32[64,1024]{1,0:T(8,128)S(1)}, f32[64,1024]{1,0:T(8,128)}, u32[]{:S(2)}) copy-start(f32[64,1024]{1,0:T(8,128)} %get-tuple-element.42) | copy-start | bytes 786436
  152.3 0.8 copy-start.6
  153.1 0.7 copy-start.7

commit v4 on v3

--- a/solution.py
+++ b/solution.py
@@ -592,35 +592,36 @@
 
     HEAD_ = g.HEAD
     lane_row = lax.broadcasted_iota(jnp.int32, (1, B), 1)
-    known = lax.broadcasted_iota(jnp.int32, (B, Q), 0) < T
-
-    def attend(i):
-        q_i, do_i = s.qs[px(i), :], s.doj[px(i), :]
-        q_m, do_m, low, slope, mixed, back = [], [], [], [], [], []
+    span = 2 * Q
+    known = lax.broadcasted_iota(jnp.int32, (B, span), 0) < T
+    keeps = [jnp.where(lax.div(lane_row, HEAD_) == h, 1.0, 0.0).astype(bf16) for h in range(B // HEAD_)]
+
+    def attend(i, carry):
+        at = rows_at(i * span, span, span)
+        q_i, do_i = s.qs[at, :], s.doj[at, :]
+        q_m = jnp.concatenate([q_i * keep for keep in keeps], axis=0)
+        do_m = jnp.concatenate([do_i * keep for keep in keeps], axis=0)
+        all_scores, all_dp = mm_t(s.Kb[...], q_m), mm_t(s.Vb[...], do_m)
+        low, slope, mixed, back = [], [], [], []
         for h in range(B // HEAD_):
-            keep = jnp.where(lax.div(lane_row, HEAD_) == h, 1.0, 0.0).astype(bf16)
-            qm, dom = q_i * keep, do_i * keep
-            scores = mm_t(s.Kb[...], qm)
+            scores = all_scores[:, h * span : (h + 1) * span]
             scores = jnp.concatenate([scores[:P], jnp.where(known, scores[P:], -1e30)], axis=0)
-            top = jnp.max(scores, axis=0, keepdims=True)
-            e = jnp.exp(scores - top)
+            e = jnp.exp(scores - jnp.max(scores, axis=0, keepdims=True))
             probs = e * (1.0 / jnp.sum(e, axis=0, keepdims=True))
             pb = probs.astype(bf16)
             mixed.append(mm(s.VT[h * HEAD_ : (h + 1) * HEAD_, :], pb))
-            dp = mm_t(s.Vb[...], dom)
-            inner = jnp.sum(dp * probs, axis=0, keepdims=True)
-            ds = (probs * (dp - inner)).astype(bf16)
+            dp = all_dp[:, h * span : (h + 1) * span]
+            ds = (probs * (dp - jnp.sum(dp * probs, axis=0, keepdims=True))).astype(bf16)
             back.append(mm(s.KT[h * HEAD_ : (h + 1) * HEAD_, :], ds))
-            q_m.append(qm)
-            do_m.append(dom)
             low.append(pb)
             slope.append(ds)
-        s.dV[...] += mm(jnp.concatenate(low, axis=1), jnp.concatenate(do_m, axis=0))
-        s.dK[...] += mm(jnp.concatenate(slope, axis=1), jnp.concatenate(q_m, axis=0))
-        s.O[yy, px(i), lanes(cc)] = jnp.concatenate(mixed, axis=0).T.astype(bf16)
-        s.dqkv[0, px(i), :] = (jnp.concatenate(back, axis=0).T * g.FACTOR).astype(bf16)
-
-    each(attend)
+        s.dV[...] += mm(jnp.concatenate(low, axis=1), do_m)
+        s.dK[...] += mm(jnp.concatenate(slope, axis=1), q_m)
+        s.O[yy, at, lanes(cc)] = jnp.concatenate(mixed, axis=0).T.astype(bf16)
+        s.dqkv[0, at, :] = (jnp.concatenate(back, axis=0).T * g.FACTOR).astype(bf16)
+        return carry
+
+    lax.fori_loop(0, P // span, attend, 0)
     o_state = gather_start(s.O.at[yy, :, lanes(cc)])
 
     def grads_kv(i):
@@ -911,6 +912,12 @@
     assert wires.used[0] <= g.copies[0] and wires.used[1] <= g.copies[1], wires.used
 
 
+def hand_over(*refs):
+    count = len(refs) // 2
+    for k in range(count):
+        refs[count + k][...] = refs[k][...].astype(refs[count + k].dtype)
+
+
 def fused(
     image, cond, context, w_conv1, w_conv2, w_embed, w_qkv, w_context, w_out, vectors, cotangent
 ):
@@ -949,6 +956,10 @@
         image.reshape(rows, chans), cond, context[0], w_conv1, w_conv2, w_embed, w_qkv, w_context, w_out, vectors,
         cotangent.reshape(rows, chans),
     )
+    count = len(outs)
+    result = pl.pallas_call(
+        hand_over, out_shape=outs, in_specs=[vmem] * count, out_specs=[vmem] * count,
+    )(*result)
     return (result[0].reshape(image.shape), result[1].reshape(image.shape), *result[2:])
 
 

time: 155 us -> 142 us (0.916)
  local copies, waits for them, and re-layouts: 8.56 us -> 0 us
  Pallas kernels: 145 us -> 141 us
    unnamed x25 -> x0, local copies, waits for them, and re-layouts: 8.56 us -> none
    pallas_call x1, Pallas kernels: 145 us -> 139 us  [fused(): pl.pallas_call(functools.partial(body, g, groups), out_shape=outs, in_spe...]
    pallas_call x0 -> x1, Pallas kernels: none -> 2.64 us  [fused(): pl.pallas_call(hand_over, out_shape=outs, in_specs=[vmem] * count, out_sp...]
where the time goes in v4:
time: 142 us
  Pallas kernels  141 us (99%)
    pallas_call x1, Pallas kernels, fused(): pl.pallas_call(functools.partial(body, g, groups), out_shape=outs, in_spe...  139 us

profile of v4, /device:TPU:0, one launch (start us, length us, event | category | flops | bytes accessed | tf_op | source)
XLA Modules:
  0.0 142.0 jit_solution(1235273372105424079)
XLA Ops:
  0.6 138.7 %shard_map.178 = (bf16[256,512]{1,0:T(8,128)(2,1)}, bf16[256,512]{1,0:T(8,128)(2,1)}, f32[144,512]{1,0:T(8,128)}, f32[144,512]{1,0:T(8,128)}, f32[64,1024]{1,0:T...) custom-call(bf16[256,512]{1,0:T(8,128)(2,1)} %bitcast.6, ...), custom_call_target="tpu_custom_call" | custom-call | tf_op jit(solution)/shard_map/pallas_call | solution.py:945
  139.4 2.6 %shard_map.179 = (bf16[256,512]{1,0:T(8,128)(2,1)}, bf16[256,512]{1,0:T(8,128)(2,1)}, f32[144,512]{1,0:T(8,128)}, f32[144,512]{1,0:T(8,128)}, f32[64,1024]{1,0:T...) custom-call(bf16[256,512]{1,0:T(8,128)(2,1)} %get-tuple-element.27.refs_0_, ...), custom_call_target="tpu_custom_call" | custom-call | tf_op jit(solution)/shard_map/pallas_call | solution.py:960

commit v5 on v4

--- a/solution.py
+++ b/solution.py
@@ -209,13 +209,19 @@
         spread = each(lambda i, a: a + colsum(jnp.square(load(i) - mean)), zero_row)
         return mean, lax.rsqrt(group_sum(spread) * (1.0 / count) + 1e-05)
 
-    col = lax.rem(lax.broadcasted_iota(jnp.int32, (Q, B), 0), COLS)
+    def column_of(v):
+        return lax.rem(lax.broadcasted_iota(jnp.int32, v.shape, 0), COLS)
 
     def from_left(v):
-        return jnp.where(col == 0, 0.0, pltpu.roll(v, 1, 0))
+        return jnp.where(column_of(v) == 0, 0.0, pltpu.roll(v, 1, 0))
 
     def from_right(v):
-        return jnp.where(col == COLS - 1, 0.0, pltpu.roll(v, Q - 1, 0))
+        return jnp.where(column_of(v) == COLS - 1, 0.0, pltpu.roll(v, v.shape[0] - 1, 0))
+
+    BIG = 2 * Q
+
+    def big(i):
+        return pl.ds(i * BIG, BIG)
 
     hot = lax.broadcasted_iota(jnp.int32, (16, C), 1) == (
         lax.broadcasted_iota(jnp.int32, (16, C), 0) + flat * g.VW
@@ -373,6 +379,8 @@
     s.dyj[rows_at(j * Q, Q, Q), :] = dy_in[:, lanes(j)]
     z_step(p1[:1], 1)
     z_step(p1[1:] + po, 1)
+    img_done(c2)
+    z_start(p2[:1])
 
     e_stage1.wait_recv()
     s.wemb[...] = jnp.zeros((2 * RE, 2 * C), bf16)
@@ -400,8 +408,6 @@
     stats(1)
     z_step(p1[:1], 2)
     z_step(p1[1:] + po, 2)
-    img_done(c2)
-    z_start(p2[:1])
     z_start(p2[1:])
     stats(2)
     stats(3)
@@ -423,6 +429,8 @@
 
     z_step(p1[:1], 3)
     z_step(p1[1:] + po, 3)
+    img_done(wq)
+    z_start(pq)
     for k in range(J):
         mean, inverse = s.st1[k, 0:1, :], s.st1[k, 1:2, :]
         gain, bias = s.vecs[k, 0:1, :], s.vecs[k, 1:2, :]
@@ -445,6 +453,8 @@
     each(lambda i: s.xj.__setitem__((px(i), slice(None)), s.X[i, :, lanes(j)]))
     z_step(p2[:1], 1)
     z_step(p2[1:], 1)
+    img_done(wc)
+    z_start(pc)
     e_stage3.wait_recv()
     total = s.esum[0]
     for k in range(1, J):
@@ -459,23 +469,22 @@
     arrive(p1)
 
     def convolve(A, W, emit):
-        def one(i):
+        right = jnp.concatenate(
+            [
+                jnp.concatenate([W[0, (3 * r + c) * C : (3 * r + c + 1) * C, :] for r in range(3)], axis=0)
+                for c in range(3)
+            ],
+            axis=1,
+        )
+        for i in range(P // BIG):
             left = jnp.concatenate(
-                [A[h, rows_at(i * Q + r * COLS, Q, COLS), :] for r in range(3) for h in range(2)], axis=1
-            )
-            right = jnp.concatenate(
-                [
-                    jnp.concatenate([W[0, (3 * r + c) * C : (3 * r + c + 1) * C, :] for r in range(3)], axis=0)
-                    for c in range(3)
-                ],
-                axis=1,
+                [A[h, i * BIG + r * COLS : (i + 1) * BIG + r * COLS, :] for r in range(3) for h in range(2)], axis=1
             )
             p = mm(left, right)
-            emit(i, p[:, B : 2 * B] + from_left(p[:, :B]) + from_right(p[:, 2 * B :]))
-        each(one)
-
-    def save_h1(i, v):
-        s.h1[px(i), :] = v + vec(2)
+            emit(big(i), p[:, B : 2 * B] + from_left(p[:, :B]) + from_right(p[:, 2 * B :]))
+
+    def save_h1(at, v):
+        s.h1[at, :] = v + vec(2)
 
     convolve(s.A1, c1.w, save_h1)
     mean2, inv2 = moments(lambda i: s.h1[px(i), :])
@@ -493,9 +502,26 @@
         u = u_of(i)
         s.A2[yy, rows_at(i * Q + COLS, Q, COLS), lanes(cc)] = (u * jax.nn.sigmoid(u)).astype(bf16)
 
-    each(act2)
-    inside = pl.ds(COLS, P)
-    a2_state = gather_start(s.A2.at[yy, inside, lanes(cc)])
+    def halves_out(act, place):
+        states = []
+        for i in range(P // BIG):
+            lax.fori_loop(i * BIG // Q, (i + 1) * BIG // Q, lambda n, carry: (act(n), carry)[1], 0)
+            states.append(gather_start(place(i, yy)))
+        return states
+
+    def halves_in(states, place):
+        for i, state in enumerate(states):
+            gather_far(state, place(i, 1 - yy))
+
+    def halves_end(states):
+        for state in states:
+            gather_near(state)
+            gather_end(state)
+
+    def a2_at(i, half):
+        return s.A2.at[half, pl.ds(COLS + i * BIG, BIG), lanes(cc)]
+
+    a2_state = halves_out(act2, a2_at)
     for h in range(2):
         part = mm_t(dy_in[:, 0 : 2 * B], s.WoF[0, h * 2 * B : (h + 1) * 2 * B, :])
         part = part + mm_t(dy_in[:, 2 * B : 4 * B], s.WoF[1, h * 2 * B : (h + 1) * 2 * B, :])
@@ -507,22 +533,20 @@
     s.doj[rows_at(j * Q, Q, Q), :] = s.dopx[:, lanes(j)]
     z_step(p2[:1], 2)
     z_step(p2[1:], 2)
-    img_done(wq)
-    img_done(wc)
-    z_start(pq)
-    z_start(pc)
+    z_step(pq, 1)
     z_step(p2[:1], 3)
     z_step(p2[1:], 3)
-    gather_far(a2_state, s.A2.at[1 - yy, inside, lanes(cc)])
+    z_step(pc, 1)
+    z_step(pq, 2)
+    halves_in(a2_state, a2_at)
     turn(s.A1, s.A1T, COLS)
-    z_step(pq, 1)
-    z_step(pc, 1)
-    gather_near(a2_state)
-    gather_end(a2_state)
+    halves_end(a2_state)
+    z_step(pc, 2)
+    z_step(pq, 3)
     arrive(p2)
 
-    def save_y1(i, v):
-        s.y1[px(i), :] = s.xj[px(i), :].astype(f32) + v + vec(5)
+    def save_y1(at, v):
+        s.y1[at, :] = s.xj[at, :].astype(f32) + v + vec(5)
 
     convolve(s.A2, c2.w, save_y1)
     mean3, inv3 = moments(lambda i: s.y1[px(i), :])
@@ -533,10 +557,10 @@
     def act3(i):
         s.N3[yy, px(i), lanes(cc)] = (xh3(i) * vec(6) + vec(7)).astype(bf16)
 
-    each(act3)
-    n_state = gather_start(s.N3.at[yy, :, lanes(cc)])
-    z_step(pq, 2)
-    z_step(pc, 2)
+    def n_at(i, half):
+        return s.N3.at[half, big(i), lanes(cc)]
+
+    n_state = halves_out(act3, n_at)
     turn(s.A2, s.A2T, COLS)
 
     def turn_weights(W, target, taps, stride):
@@ -549,9 +573,8 @@
         return lambda t: W.w.at[0, pl.ds(t * C, C), :]
 
     turn_weights(conv_tap(c2), s.W2T, 9, C)
-    gather_far(n_state, s.N3.at[1 - yy, :, lanes(cc)])
-    z_step(pq, 3)
     z_step(pc, 3)
+    halves_in(n_state, n_at)
     turn_weights(conv_tap(c1), s.W1T, 9, C)
     arrive(pq)
     arrive(pc)
@@ -560,8 +583,7 @@
     for t, target in enumerate((s.Kb, s.Vb)):
         v = mm(s.ctx[...], wc.w[t]) + vec(12 + t)
         target[P : P + B, :] = jnp.where(tokens, v, 0.0).astype(bf16)
-    gather_near(n_state)
-    gather_end(n_state)
+    halves_end(n_state)
 
     def tokens_of(owner):
         return s.ctx.at[0:TP, rows_at(owner * XN, XN, B)]
@@ -572,16 +594,17 @@
     )
     s.ctxs[d, 0:TP, :] = tokens_of(d)[...]
 
-    def project(i):
-        left = jnp.concatenate([s.N3[0, px(i), :], s.N3[1, px(i), :]], axis=1)
+    def project(at):
+        left = jnp.concatenate([s.N3[0, at, :], s.N3[1, at, :]], axis=1)
         right = jnp.concatenate([wq.w[t] for t in range(3)], axis=1)
         v = mm(left, right)
         q = (v[:, :B] + vec(9)).astype(bf16)
-        s.qs[px(i), :] = (q.astype(f32) * g.FACTOR).astype(bf16)
-        s.Kb[px(i), :] = (v[:, B : 2 * B] + vec(10)).astype(bf16)
-        s.Vb[px(i), :] = (v[:, 2 * B :] + vec(11)).astype(bf16)
-
-    each(project)
+        s.qs[at, :] = (q.astype(f32) * g.FACTOR).astype(bf16)
+        s.Kb[at, :] = (v[:, B : 2 * B] + vec(10)).astype(bf16)
+        s.Vb[at, :] = (v[:, 2 * B :] + vec(11)).astype(bf16)
+
+    for i in range(P // BIG):
+        project(big(i))
     for source, target in ((s.Kb, s.KT), (s.Vb, s.VT)):
         for k in range(0, P + B, B):
             target[:, k : k + B] = source[k : k + B, :].T
@@ -596,8 +619,8 @@
     known = lax.broadcasted_iota(jnp.int32, (B, span), 0) < T
     keeps = [jnp.where(lax.div(lane_row, HEAD_) == h, 1.0, 0.0).astype(bf16) for h in range(B // HEAD_)]
 
-    def attend(i, carry):
-        at = rows_at(i * span, span, span)
+    def attend(i):
+        at = pl.ds(i * span, span)
         q_i, do_i = s.qs[at, :], s.doj[at, :]
         q_m = jnp.concatenate([q_i * keep for keep in keeps], axis=0)
         do_m = jnp.concatenate([do_i * keep for keep in keeps], axis=0)
@@ -619,10 +642,9 @@
         s.dK[...] += mm(jnp.concatenate(slope, axis=1), q_m)
         s.O[yy, at, lanes(cc)] = jnp.concatenate(mixed, axis=0).T.astype(bf16)
         s.dqkv[0, at, :] = (jnp.concatenate(back, axis=0).T * g.FACTOR).astype(bf16)
-        return carry
-
-    lax.fori_loop(0, P // span, attend, 0)
-    o_state = gather_start(s.O.at[yy, :, lanes(cc)])
+        return gather_start(s.O.at[yy, at, lanes(cc)])
+
+    o_states = [attend(i) for i in range(P // span)]
 
     def grads_kv(i):
         s.dqkv[1, px(i), :] = s.dK[px(i), :].astype(bf16)
@@ -632,30 +654,36 @@
 
     def scatter(bufs, left, right):
         ps, rc, sy, ry = bufs.ps, bufs.rc, bufs.sy, bufs.ry
-        near = []
-        for slot in range(2):
-            half = 1 - yy if slot == 0 else yy
-
-            def one(i):
-                v = mm(left(i), right[half]).astype(bf16)
-                ps[slot, 0, px(i), :] = v[:, :B]
-                ps[slot, 1, px(i), :] = v[:, B:]
-
-            each(one)
-            near.append(send(ps.at[slot, 1 - cc], rc.at[slot], sib))
-            if slot == 0:
-                near[0].wait_recv()
-
-                def add(i):
-                    v = ps[0, cc, px(i), :].astype(f32) + rc[0, px(i), :].astype(f32)
-                    sy[px(i), :] = v.astype(bf16)
-
-                each(add)
-                across = send(sy, ry, ypeer)
+        near, y_in = [], []
+        part = BIG // Q
+
+        def halves_of(slot, half):
+            other = 1 - yy if slot == 0 else yy
+
+            at = big(half)
+            v = mm(left(half * BIG, BIG), right[other]).astype(bf16)
+            ps[slot, 0, at, :] = v[:, :B]
+            ps[slot, 1, at, :] = v[:, B:]
+            return send(ps.at[slot, 1 - cc, at, :], rc.at[slot, at, :], sib)
+
+        far = [halves_of(0, half) for half in range(P // BIG)]
+        for half in range(P // BIG):
+            near.append(halves_of(1, half))
+            far[half].wait_recv()
+
+            def add(n, carry):
+                i = n + half * part
+                v = ps[0, cc, px(i), :].astype(f32) + rc[0, px(i), :].astype(f32)
+                sy[px(i), :] = v.astype(bf16)
+                return carry
+
+            lax.fori_loop(0, part, add, 0)
+            at = big(half)
+            y_in.append(send(sy.at[at, :], ry.at[at, :], ypeer))
 
         def done():
-            near[1].wait_recv()
-            across.wait_recv()
+            for copy in near + y_in:
+                copy.wait_recv()
 
         def load(i):
             v = ps[1, cc, px(i), :].astype(f32) + rc[1, px(i), :].astype(f32)
@@ -663,7 +691,7 @@
 
         return done, load
 
-    order = list(range(1, Z)) + [0]
+    order = sorted(range(1, Z), key=lambda k: -min(k, Z - k)) + [0]
 
     def sum_start(W):
         W.sx, W.zout, W.zin = {}, wires.slot(0), wires.slot(1)
@@ -712,7 +740,7 @@
                 target[:, t * C + k * B : t * C + (k + 1) * B] = W.gr[k, t].astype(f32)
 
     dn_done, dn_at = scatter(
-        dn_bufs, lambda i: jnp.concatenate([s.dqkv[t, px(i), :] for t in range(3)], axis=1), s.WqT
+        dn_bufs, lambda at, size: jnp.concatenate([s.dqkv[t, pl.ds(at, size), :] for t in range(3)], axis=1), s.WqT
     )
     turn(s.N3, s.N3T, 0)
     for h in range(2):
@@ -727,15 +755,18 @@
         [(s.dcx.at[0:TP, :], s.dcxs.at[d, 0:TP, :], device) for device in dp_peers],
         s.dcxs.at[0 : N - 1, 0:TP, :],
     )
-    gather_far(o_state, s.O.at[1 - yy, :, lanes(cc)])
-    gather_near(o_state)
-    gather_end(o_state)
-
-    def finish(i):
-        left = jnp.concatenate([s.O[0, px(i), :], s.O[1, px(i), :]], axis=1)
-        s.outj[px(i), :] = (s.y1[px(i), :] + mm(left, wo.w[0]) + vec(8)).astype(bf16)
-
-    each(finish)
+    for i, state in enumerate(o_states):
+        gather_far(state, s.O.at[1 - yy, pl.ds(i * span, span), lanes(cc)])
+    for state in o_states:
+        gather_near(state)
+        gather_end(state)
+
+    def finish(at):
+        left = jnp.concatenate([s.O[0, at, :], s.O[1, at, :]], axis=1)
+        s.outj[at, :] = (s.y1[at, :] + mm(left, wo.w[0]) + vec(8)).astype(bf16)
+
+    for i in range(P // BIG):
+        finish(big(i))
 
     def to_pixels(source, target):
         copies = group(
@@ -783,8 +814,8 @@
         r, c = t // 3, t % 3
         return s.S[c, rows_at(start + (2 - r) * COLS, size, COLS), :]
 
-    def field(i):
-        return jnp.concatenate([tap(t, i * Q, Q) for t in range(9)], axis=1)
+    def field(at, size):
+        return jnp.concatenate([tap(t, at, size) for t in range(9)], axis=1)
 
     def kernel_grad(W, turned):
         for h in range(2):
@@ -839,6 +870,7 @@
     ds_copies.wait_recv()
     s.dsall[d] = s.dse[...]
     ds_copies = group([(s.dse, s.dsall.at[d], device) for device in dp_peers], s.dsall.at[0 : N - 1])
+    sum_block(c1, order[0])
     da1_done()
     mean1, inv1 = s.st1[j, 0:1, :], s.st1[j, 1:2, :]
 
@@ -852,6 +884,7 @@
         return carry[0] + colsum(dt1), carry[1] + colsum(dt1 * n1)
 
     dt1_sum, dt1_hat = each(make_dt1, (zero_row, zero_row))
+    sum_block(c1, order[1])
     m1c = group_sum(dt1_sum * vec(0)) * (1.0 / count)
     m2c = group_sum(dt1_hat * vec(0)) * (1.0 / count)
 
@@ -871,7 +904,8 @@
     )
     gv_copies = group([(s.gvec, s.gvs.at[d], device) for device in dp_peers], s.gvs.at[0 : N - 1])
     s.gvs[d] = s.gvec[...]
-    sum_z(c1)
+    for k in order[2:]:
+        sum_block(c1, k)
     gv_copies.wait_recv()
     total = s.gvs[0]
     for k in range(1, N):
@@ -940,7 +974,7 @@
         shape(w_embed.shape, f32), shape(w_qkv.shape, f32), shape(w_context.shape, f32), shape(w_out.shape, f32),
         shape(vectors.shape, f32),
     ]
-    g.copies = (71, 49 + 11 * (N // 2 + 1))
+    g.copies = (89, 67 + 11 * (N // 2 + 1))
     vmem = pl.BlockSpec(memory_space=pltpu.VMEM)
     result = pl.pallas_call(
         functools.partial(body, g, groups),

time: 142 us -> 139 us (0.979); the launches traced: 142 us -> 137 us
  Pallas kernels: 141 us -> 137 us
    pallas_call x1, Pallas kernels: 139 us -> 134 us  [fused(): pl.pallas_call(functools.partial(body, g, groups), out_shape=outs, in_spe...]
where the time goes in v5:
time: 139 us; the launch traced here: 137 us
  Pallas kernels  137 us (99%)
    pallas_call x1, Pallas kernels, fused(): pl.pallas_call(functools.partial(body, g, groups), out_shape=outs, in_spe...  134 us

profile of v5, /device:TPU:0, one launch (start us, length us, event | category | flops | bytes accessed | tf_op | source)
XLA Modules:
  0.0 137.3 jit_solution(9176026832709835970)
XLA Ops:
  0.6 134.0 %shard_map.178 = (bf16[256,512]{1,0:T(8,128)(2,1)}, bf16[256,512]{1,0:T(8,128)(2,1)}, f32[144,512]{1,0:T(8,128)}, f32[144,512]{1,0:T(8,128)}, f32[64,1024]{1,0:T...) custom-call(bf16[256,512]{1,0:T(8,128)(2,1)} %bitcast.6, ...), custom_call_target="tpu_custom_call" | custom-call | tf_op jit(solution)/shard_map/pallas_call | solution.py:979
  134.7 2.6 %shard_map.179 = (bf16[256,512]{1,0:T(8,128)(2,1)}, bf16[256,512]{1,0:T(8,128)(2,1)}, f32[144,512]{1,0:T(8,128)}, f32[144,512]{1,0:T(8,128)}, f32[64,1024]{1,0:T...) custom-call(bf16[256,512]{1,0:T(8,128)(2,1)} %get-tuple-element.27.refs_0_, ...), custom_call_target="tpu_custom_call" | custom-call | tf_op jit(solution)/shard_map/pallas_call | solution.py:994

commit v6 on v5

--- a/solution.py
+++ b/solution.py
@@ -914,6 +914,7 @@
     s.gvi[j] = total
     gv_copies = group([(s.gvt, s.gvi.at[j], device) for device in img_peers], s.gvi.at[0 : J - 1])
     sum_img(c2)
+    sum_img(c1)
     sum_end(wq, g_q)
     sum_end(wc, g_c)
     sum_end(wo, g_o)
@@ -938,7 +939,6 @@
         preferred_element_type=f32,
     )
     sum_end(c2, gc2)
-    sum_img(c1)
     sum_end(c1, gc1)
     out_copies.wait_recv()
     in_copies.wait_recv()

time: 139 us -> 137 us (0.986)
  no operation moved by 1% of the time
where the time goes in v6:
time: 137 us; the launch traced here: 136 us
  Pallas kernels  136 us (99%)
    pallas_call x1, Pallas kernels, fused(): pl.pallas_call(functools.partial(body, g, groups), out_shape=outs, in_spe...  133 us

profile of v6, /device:TPU:0, one launch (start us, length us, event | category | flops | bytes accessed | tf_op | source)
XLA Modules:
  0.0 136.5 jit_solution(16684768256930887987)
XLA Ops:
  0.6 133.2 %shard_map.178 = (bf16[256,512]{1,0:T(8,128)(2,1)}, bf16[256,512]{1,0:T(8,128)(2,1)}, f32[144,512]{1,0:T(8,128)}, f32[144,512]{1,0:T(8,128)}, f32[64,1024]{1,0:T...) custom-call(bf16[256,512]{1,0:T(8,128)(2,1)} %bitcast.6, ...), custom_call_target="tpu_custom_call" | custom-call | tf_op jit(solution)/shard_map/pallas_call | solution.py:979
  133.8 2.6 %shard_map.179 = (bf16[256,512]{1,0:T(8,128)(2,1)}, bf16[256,512]{1,0:T(8,128)(2,1)}, f32[144,512]{1,0:T(8,128)}, f32[144,512]{1,0:T(8,128)}, f32[64,1024]{1,0:T...) custom-call(bf16[256,512]{1,0:T(8,128)(2,1)} %get-tuple-element.27.refs_0_, ...), custom_call_target="tpu_custom_call" | custom-call | tf_op jit(solution)/shard_map/pallas_call | solution.py:994

commit v7 on v6

--- a/solution.py
+++ b/solution.py
@@ -315,7 +315,9 @@
         half = W.depth // 32 * 16
         return [piece(W, 0, half), piece(W, half, W.depth - half)]
 
-    p1, p2 = halves(c1), halves(c2)
+    third = c1.depth // 48 * 16
+    p1 = [piece(c1, 0, third), piece(c1, third, third), piece(c1, 2 * third, c1.depth - 2 * third)]
+    p2 = halves(c2)
     pq, pc, po = ([piece(W, 0, W.depth)] for W in rest)
 
     def gather_start(mine):
@@ -974,7 +976,7 @@
         shape(w_embed.shape, f32), shape(w_qkv.shape, f32), shape(w_context.shape, f32), shape(w_out.shape, f32),
         shape(vectors.shape, f32),
     ]
-    g.copies = (89, 67 + 11 * (N // 2 + 1))
+    g.copies = (91, 67 + 12 * (N // 2 + 1))
     vmem = pl.BlockSpec(memory_space=pltpu.VMEM)
     result = pl.pallas_call(
         functools.partial(body, g, groups),

time: 137 us -> 137 us (level)
  no operation moved by 1% of the time
where the time goes in v7:
time: 137 us
  Pallas kernels  136 us (99%)
    pallas_call x1, Pallas kernels, fused(): pl.pallas_call(functools.partial(body, g, groups), out_shape=outs, in_spe...  133 us

profile of v7, /device:TPU:0, one launch (start us, length us, event | category | flops | bytes accessed | tf_op | source)
XLA Modules:
  0.0 136.6 jit_solution(14654252734290992163)
XLA Ops:
  0.6 133.3 %shard_map.178 = (bf16[256,512]{1,0:T(8,128)(2,1)}, bf16[256,512]{1,0:T(8,128)(2,1)}, f32[144,512]{1,0:T(8,128)}, f32[144,512]{1,0:T(8,128)}, f32[64,1024]{1,0:T...) custom-call(bf16[256,512]{1,0:T(8,128)(2,1)} %bitcast.6, ...), custom_call_target="tpu_custom_call" | custom-call | tf_op jit(solution)/shard_map/pallas_call | solution.py:981
  133.9 2.6 %shard_map.179 = (bf16[256,512]{1,0:T(8,128)(2,1)}, bf16[256,512]{1,0:T(8,128)(2,1)}, f32[144,512]{1,0:T(8,128)}, f32[144,512]{1,0:T(8,128)}, f32[64,1024]{1,0:T...) custom-call(bf16[256,512]{1,0:T(8,128)(2,1)} %get-tuple-element.27.refs_0_, ...), custom_call_target="tpu_custom_call" | custom-call | tf_op jit(solution)/shard_map/pallas_call | solution.py:996
